TPU v7x, 32 devices: a whole 2x2x4 slice. The times are simulated.
32 devices in a mesh: dp: 8 (over z, y), tensor: 4 (over x, core).
Axes of the slice: x: 2, y: 2, z: 4, core: 2. Of those that a mesh axis runs over, the one named last changes fastest.
Arguments:
- query_tokens: bfloat16 [8192, 768], P(('dp', 'tensor')), may hold values from -6 to 6
- key_tokens: bfloat16 [8192, 768], P(('dp', 'tensor')), may hold values from -6 to 6
- query_lengths: int32 [32], P('dp'), may hold values from 64 to 256, as said below
- key_lengths: int32 [32], P('dp'), may hold values from 64 to 256, as said below
- positives: int32 [32], replicated, may hold values from 0 to 31, each once
- key_queue: bfloat16 [16384, 768], P(('dp', 'tensor')), may hold values from -0.59765625 to 0.59765625
- token_cotangent: bfloat16 [8192, 768], P(('dp', 'tensor')), may hold values from -0.0059814453 to 0.0059814453
- heads_in: bfloat16 [3, 768, 768], P(None, None, 'tensor'), may hold values from -0.21875 to 0.21875
- heads_bias: bfloat16 [2, 768], P(None, 'tensor'), may hold values from -1.796875 to 1.796875
- heads_out: bfloat16 [768, 768], P('tensor'), may hold values from -1.25 to 1.25
- expand_weight: bfloat16 [768, 3072], P(None, 'tensor'), may hold values from -0.21875 to 0.21875
- expand_bias: bfloat16 [3072], replicated, may hold values from -1.796875 to 1.796875
- shrink_weight: bfloat16 [3072, 768], P('tensor'), may hold values from -0.109375 to 0.109375
- branch_bias: bfloat16 [2, 768], replicated, may hold values from -1.796875 to 1.796875
- norm_gain: bfloat16 [2, 768], replicated, may hold values from 0.099609375 to 1.8984375
- norm_shift: bfloat16 [2, 768], replicated, may hold values from -0.59765625 to 0.59765625
- momentum_heads_in: float32 [3, 768, 768], P(None, 'dp', 'tensor'), may hold values from -0.21875 to 0.21875
- momentum_heads_bias: float32 [2, 768], P(None, 'tensor'), may hold values from -1.8 to 1.8
- momentum_heads_out: float32 [768, 768], P('tensor', 'dp'), may hold values from -1.25 to 1.25
- momentum_expand_weight: float32 [768, 3072], P('dp', 'tensor'), may hold values from -0.21875 to 0.21875
- momentum_expand_bias: float32 [3072], replicated, may hold values from -1.8 to 1.8
- momentum_shrink_weight: float32 [3072, 768], P('tensor', 'dp'), may hold values from -0.109375 to 0.109375
- momentum_branch_bias: float32 [2, 768], replicated, may hold values from -1.8 to 1.8
- momentum_norm_gain: float32 [2, 768], replicated, may hold values from 0.4 to 1.6
- momentum_norm_shift: float32 [2, 768], replicated, may hold values from -0.6 to 0.6
Outputs:
- query_output: bfloat16 [8192, 768], P(('dp', 'tensor'))
- key_output: bfloat16 [8192, 768], P(('dp', 'tensor'))
- contrast_loss: float32 [], replicated
- input_gradient: float32 [8192, 768], P(('dp', 'tensor'))
- gradient_heads_in: float32 [3, 768, 768], P(None, None, 'tensor')
- gradient_heads_bias: float32 [2, 768], P(None, 'tensor')
- gradient_heads_out: float32 [768, 768], P('tensor')
- gradient_expand_weight: float32 [768, 3072], P(None, 'tensor')
- gradient_expand_bias: float32 [3072], P('tensor')
- gradient_shrink_weight: float32 [3072, 768], P('tensor')
- gradient_branch_bias: float32 [2, 768], replicated
- gradient_norm_gain: float32 [2, 768], replicated
- gradient_norm_shift: float32 [2, 768], replicated
- updated_heads_in: float32 [3, 768, 768], P(None, 'dp', 'tensor')
- updated_heads_bias: float32 [2, 768], P(None, 'tensor')
- updated_heads_out: float32 [768, 768], P('tensor', 'dp')
- updated_expand_weight: float32 [768, 3072], P('dp', 'tensor')
- updated_expand_bias: float32 [3072], P('tensor')
- updated_shrink_weight: float32 [3072, 768], P('tensor', 'dp')
- updated_branch_bias: float32 [2, 768], replicated
- updated_norm_gain: float32 [2, 768], replicated
- updated_norm_shift: float32 [2, 768], replicated
Inputs may be any that keep to these rules, and one draw needn't show every extreme that they name: `query_lengths`: some crop has exactly 256 valid tokens and some exactly 64. `key_lengths`: some crop has exactly 256 valid tokens and some exactly 64. `positives`: every key crop is the positive of exactly one query crop.
All inputs are finite; a program needn't handle non-finite values.
Results may differ from a plain program's by a relative error of at most 0.018.
Values may be sent and summed in bfloat16 or wider, within the bound.
A program may use at most 128 MiB of HBM per device.

v0:
```python
import jax
import jax.numpy as jnp
from jax import lax
from jax.sharding import PartitionSpec as P

HEAD = 64


SOFTMAX_DIVISOR = 0.05
MOMENTUM = 0.5
NORM_EPSILON = 1e-12
MASKED_SCORE = -1e30
ROOT_HALF = 0.7071067811865476
GAUSS_SCALE = 0.3989422804014327
CONTRACT_ROWS = (((0,), (0,)), ((), ()))
CONTRACT_COLS = (((1,), (1,)), ((), ()))


def joined(part, axis, combine):
    gathered = jax.tree.map(lambda a: lax.all_gather(a, axis), part)

    def take(source):
        return jax.tree.map(lambda a: lax.dynamic_index_in_dim(a, source, 0, False), gathered)

    return lax.fori_loop(
        1, lax.axis_size(axis), lambda source, state: combine(state, take(source)), take(0)
    )


def gather_rows(inputs):
    return lax.all_gather(inputs, "tensor", axis=0, tiled=True)


def sum_rows(inputs):
    return lax.psum_scatter(
        inputs.astype(jnp.bfloat16), "tensor", scatter_dimension=0, tiled=True
    ).astype(jnp.float32)


def gather_grads(inputs):
    return lax.all_gather(inputs, "tensor", axis=0, tiled=True)


def sum_grads(inputs):
    return lax.psum_scatter(
        inputs.astype(jnp.bfloat16), "tensor", scatter_dimension=0, tiled=True
    ).astype(jnp.float32)


def norm_rows(inputs, gain_row, shift_row):
    row_mean = jnp.mean(inputs, axis=-1, keepdims=True)
    centered = inputs - row_mean
    inverse_std = lax.rsqrt(jnp.mean(centered * centered, axis=-1, keepdims=True) + NORM_EPSILON)
    normalized = centered * inverse_std
    return (normalized * gain_row + shift_row, normalized, inverse_std)


def norm_back(upstream, normalized, inverse_std, gain_row):
    scaled = upstream * gain_row
    inner = (
        scaled
        - jnp.mean(scaled, axis=-1, keepdims=True)
        - normalized * jnp.mean(scaled * normalized, axis=-1, keepdims=True)
    )
    return (inner * inverse_std, jnp.sum(upstream * normalized, axis=0), jnp.sum(upstream, axis=0))


def gelu_parts(inputs):
    normal_cdf = 0.5 * (1.0 + lax.erf(inputs * ROOT_HALF))
    return (
        inputs * normal_cdf,
        normal_cdf + inputs * GAUSS_SCALE * jnp.exp(-0.5 * inputs * inputs),
    )


def scores_of(query_heads, key_heads, lengths):
    crops, length = (query_heads.shape[0], query_heads.shape[1])
    raw_scores = jnp.einsum(
        "cshd,cthd->chst", query_heads, key_heads, preferred_element_type=jnp.float32
    ) * HEAD ** (-0.5)
    valid_key = (
        lax.broadcasted_iota(jnp.int32, (crops, 1, 1, length), 3) < lengths[:, None, None, None]
    )
    return jnp.where(valid_key, raw_scores, MASKED_SCORE)


def forward(tokens, lengths, matrices, vectors):
    heads_in, heads_out, expand_weight, shrink_weight = matrices
    heads_bias, expand_bias, branch_bias, norm_gain, norm_shift = vectors
    crops = lengths.shape[0]
    gathered = gather_rows(tokens)
    length = gathered.shape[0] // crops
    columns = heads_in.shape[2]
    head_shape = (crops, length, columns // HEAD, HEAD)
    projected = jnp.einsum("gd,tdc->tgc", gathered, heads_in, preferred_element_type=jnp.float32)
    query_heads = (projected[0] + heads_bias[0]).astype(jnp.bfloat16).reshape(head_shape)
    key_heads = projected[1].astype(jnp.bfloat16).reshape(head_shape)
    value_heads = (projected[2] + heads_bias[1]).astype(jnp.bfloat16).reshape(head_shape)
    scores = scores_of(query_heads, key_heads, lengths)
    largest_each = jnp.max(scores, axis=-1, keepdims=True)
    powers = jnp.exp(scores - largest_each)
    power_total = jnp.sum(powers, axis=-1, keepdims=True)
    log_total = largest_each + jnp.log(power_total)
    weights_low = (powers / power_total).astype(jnp.bfloat16)
    context = jnp.einsum(
        "chst,cthd->cshd", weights_low, value_heads, preferred_element_type=jnp.float32
    )
    context = context.astype(jnp.bfloat16).reshape(crops * length, columns)
    attended = sum_rows(jnp.dot(context, heads_out, preferred_element_type=jnp.float32))
    middle, normed_one, inverse_one = norm_rows(
        tokens.astype(jnp.float32) + attended + branch_bias[0], norm_gain[0], norm_shift[0]
    )
    middle_low = middle.astype(jnp.bfloat16)
    share = expand_weight.shape[1]
    bias_part = lax.dynamic_slice_in_dim(expand_bias, lax.axis_index("tensor") * share, share, 0)
    ffn_rows = gather_rows(middle_low)
    hidden, gelu_slope = gelu_parts(
        jnp.dot(ffn_rows, expand_weight, preferred_element_type=jnp.float32) + bias_part
    )
    hidden_low = hidden.astype(jnp.bfloat16)
    branch = sum_rows(jnp.dot(hidden_low, shrink_weight, preferred_element_type=jnp.float32))
    ffn_mats = (expand_weight, shrink_weight)
    output, normed_two, inverse_two = norm_rows(
        middle + branch + branch_bias[1], norm_gain[1], norm_shift[1]
    )
    kept = (
        gathered,
        query_heads,
        key_heads,
        value_heads,
        log_total,
        context,
        ffn_rows,
        gelu_slope,
        hidden_low,
        normed_one,
        inverse_one,
        normed_two,
        inverse_two,
        ffn_mats,
    )
    return (output, kept)


def backward(d_output, lengths, matrices, norm_gain, kept):
    heads_in, heads_out = (matrices[0], matrices[1])
    (
        gathered,
        query_heads,
        key_heads,
        value_heads,
        log_total,
        context,
        ffn_rows,
        gelu_slope,
        hidden_low,
        normed_one,
        inverse_one,
        normed_two,
        inverse_two,
        ffn_mats,
    ) = kept
    ffn_expand, ffn_shrink = ffn_mats
    d_second, gain_two, shift_two = norm_back(d_output, normed_two, inverse_two, norm_gain[1])
    d_second_low = d_second.astype(jnp.bfloat16)
    d_branch = gather_grads(d_second_low)
    grad_shrink = lax.dot_general(
        hidden_low, d_branch, CONTRACT_ROWS, preferred_element_type=jnp.float32
    )
    d_hidden = lax.dot_general(
        d_branch, ffn_shrink, CONTRACT_COLS, preferred_element_type=jnp.float32
    )
    d_pre = (d_hidden * gelu_slope).astype(jnp.bfloat16)
    grad_expand = lax.dot_general(
        ffn_rows, d_pre, CONTRACT_ROWS, preferred_element_type=jnp.float32
    )
    grad_expand_bias = jnp.sum(d_pre.astype(jnp.float32), axis=0)
    d_middle = d_second + sum_grads(
        lax.dot_general(d_pre, ffn_expand, CONTRACT_COLS, preferred_element_type=jnp.float32)
    )
    d_mixed, gain_one, shift_one = norm_back(d_middle, normed_one, inverse_one, norm_gain[0])
    d_attended = gather_grads(d_mixed.astype(jnp.bfloat16))
    grad_heads_out = lax.dot_general(
        context, d_attended, CONTRACT_ROWS, preferred_element_type=jnp.float32
    )
    d_context = lax.dot_general(
        d_attended, heads_out, CONTRACT_COLS, preferred_element_type=jnp.float32
    )
    d_context = d_context.astype(jnp.bfloat16).reshape(query_heads.shape)
    weights = jnp.exp(scores_of(query_heads, key_heads, lengths) - log_total)
    d_weights = jnp.einsum(
        "cshd,cthd->chst", d_context, value_heads, preferred_element_type=jnp.float32
    )
    inner = jnp.sum(d_weights * weights, axis=-1, keepdims=True)
    d_scores = (weights * (d_weights - inner) * HEAD ** (-0.5)).astype(jnp.bfloat16)
    d_query = jnp.einsum(
        "chst,cthd->cshd", d_scores, key_heads, preferred_element_type=jnp.float32
    ).astype(jnp.bfloat16)
    d_key = jnp.einsum(
        "chst,cshd->cthd", d_scores, query_heads, preferred_element_type=jnp.float32
    ).astype(jnp.bfloat16)
    d_value = jnp.einsum(
        "chst,cshd->cthd",
        weights.astype(jnp.bfloat16),
        d_context,
        preferred_element_type=jnp.float32,
    ).astype(jnp.bfloat16)
    d_heads = jnp.stack([d_query, d_key, d_value]).reshape(3, gathered.shape[0], heads_in.shape[2])
    grad_heads_in = jnp.einsum("gd,tgc->tdc", gathered, d_heads, preferred_element_type=jnp.float32)
    grad_heads_bias = jnp.sum(d_heads[0::2].astype(jnp.float32), axis=1)
    d_tokens = d_mixed + sum_grads(
        jnp.einsum("tgc,tdc->gd", d_heads, heads_in, preferred_element_type=jnp.float32)
    )
    grad_heads_in, grad_heads_bias, grad_heads_out, grad_expand, grad_expand_bias, grad_shrink = (
        lax.psum(
            (
                grad_heads_in,
                grad_heads_bias,
                grad_heads_out,
                grad_expand,
                grad_expand_bias,
                grad_shrink,
            ),
            "dp",
        )
    )
    bias_pair = jnp.stack([jnp.sum(d_mixed, axis=0), jnp.sum(d_second, axis=0)])
    grad_bias, grad_gain, grad_shift = lax.psum(
        (bias_pair, jnp.stack([gain_one, gain_two]), jnp.stack([shift_one, shift_two])),
        ("dp", "tensor"),
    )
    return (
        d_tokens,
        (
            grad_heads_in,
            grad_heads_bias,
            grad_heads_out,
            grad_expand,
            grad_expand_bias,
            grad_shrink,
            grad_bias,
            grad_gain,
            grad_shift,
        ),
    )


def pool_rows(output, lengths):
    crops = lengths.shape[0]
    length = output.shape[0] // crops
    shaped = output.reshape(crops, length, output.shape[1])
    mask = (lax.broadcasted_iota(jnp.int32, (crops, length), 1) < lengths[:, None]).astype(
        jnp.float32
    )
    return (jnp.sum(shaped * mask[:, :, None], axis=1) / lengths[:, None].astype(jnp.float32), mask)


def unit_rows(pooled):
    inverse = lax.rsqrt(jnp.sum(pooled * pooled, axis=-1, keepdims=True) + 1e-06)
    return (pooled * inverse, inverse)


def merge_stats(first, second):
    peak = jnp.maximum(first[0], second[0])
    return (peak, first[1] * jnp.exp(first[0] - peak) + second[1] * jnp.exp(second[0] - peak))


def blend(old_value, new_value):
    return MOMENTUM * old_value + (1.0 - MOMENTUM) * new_value.astype(jnp.float32)


def local(
    query_tokens,
    key_tokens,
    query_lengths,
    key_lengths,
    positives,
    key_queue,
    token_cotangent,
    heads_in,
    heads_bias,
    heads_out,
    expand_weight,
    expand_bias,
    shrink_weight,
    branch_bias,
    norm_gain,
    norm_shift,
    momentum_heads_in,
    momentum_heads_bias,
    momentum_heads_out,
    momentum_expand_weight,
    momentum_expand_bias,
    momentum_shrink_weight,
    momentum_branch_bias,
    momentum_norm_gain,
    momentum_norm_shift,
):
    tensor_size = lax.axis_size("tensor")
    tensor_at = lax.axis_index("tensor")
    data_at = lax.axis_index("dp")
    share = momentum_heads_in.shape[1]
    ff_share = expand_weight.shape[1]
    updated = (
        blend(momentum_heads_in, lax.dynamic_slice_in_dim(heads_in, data_at * share, share, 1)),
        blend(momentum_heads_bias, heads_bias),
        blend(momentum_heads_out, lax.dynamic_slice_in_dim(heads_out, data_at * share, share, 1)),
        blend(
            momentum_expand_weight,
            lax.dynamic_slice_in_dim(expand_weight, data_at * share, share, 0),
        ),
        blend(momentum_expand_bias, expand_bias),
        blend(
            momentum_shrink_weight,
            lax.dynamic_slice_in_dim(shrink_weight, data_at * share, share, 1),
        ),
        blend(momentum_branch_bias, branch_bias),
        blend(momentum_norm_gain, norm_gain),
        blend(momentum_norm_shift, norm_shift),
    )
    key_matrices = (
        lax.all_gather(updated[0].astype(jnp.bfloat16), "dp", axis=1, tiled=True),
        lax.all_gather(updated[2].astype(jnp.bfloat16), "dp", axis=1, tiled=True),
        lax.all_gather(updated[3].astype(jnp.bfloat16), "dp", axis=0, tiled=True),
        lax.all_gather(updated[5].astype(jnp.bfloat16), "dp", axis=1, tiled=True),
    )
    key_vectors = (updated[1], updated[4], updated[6], updated[7], updated[8])
    query_matrices = (heads_in, heads_out, expand_weight, shrink_weight)
    query_vectors = (
        heads_bias.astype(jnp.float32),
        expand_bias.astype(jnp.float32),
        branch_bias.astype(jnp.float32),
        norm_gain.astype(jnp.float32),
        norm_shift.astype(jnp.float32),
    )
    own_count = query_lengths.shape[0] // tensor_size
    query_result, kept = forward(query_tokens, query_lengths, query_matrices, query_vectors)
    key_result = forward(key_tokens, key_lengths, key_matrices, key_vectors)[0]
    own_query_lengths = lax.dynamic_slice_in_dim(query_lengths, tensor_at * own_count, own_count, 0)
    own_key_lengths = lax.dynamic_slice_in_dim(key_lengths, tensor_at * own_count, own_count, 0)
    query_pooled, query_mask = pool_rows(query_result, own_query_lengths)
    key_pooled = pool_rows(key_result, own_key_lengths)[0]
    query_unit, query_inverse = unit_rows(query_pooled)
    key_unit = unit_rows(key_pooled)[0]
    all_query, all_key = (
        lax.all_gather(query_unit.astype(jnp.bfloat16), ("dp", "tensor"), axis=0, tiled=True),
        lax.all_gather(key_unit.astype(jnp.bfloat16), ("dp", "tensor"), axis=0, tiled=True),
    )
    queue_logits = (
        lax.dot_general(all_query, key_queue, CONTRACT_COLS, preferred_element_type=jnp.float32)
        / SOFTMAX_DIVISOR
    )
    largest_each = jnp.max(queue_logits, axis=1)
    power_total = jnp.sum(jnp.exp(queue_logits - largest_each[:, None]), axis=1)
    negative_max, negative_total = joined(
        (largest_each, power_total), ("dp", "tensor"), merge_stats
    )
    partner_units = jnp.take(all_key, positives, axis=0).astype(jnp.float32)
    match_score = jnp.sum(all_query.astype(jnp.float32) * partner_units, axis=1) / SOFTMAX_DIVISOR
    peak = jnp.maximum(negative_max, match_score)
    level = peak + jnp.log(
        negative_total * jnp.exp(negative_max - peak) + jnp.exp(match_score - peak)
    )
    contrast_loss = jnp.sum(level - match_score)
    scaled_weights = (jnp.exp(queue_logits - level[:, None]) / SOFTMAX_DIVISOR).astype(jnp.bfloat16)
    unit_grad = lax.psum_scatter(
        jnp.dot(scaled_weights, key_queue, preferred_element_type=jnp.float32),
        ("dp", "tensor"),
        scatter_dimension=0,
        tiled=True,
    )
    first_own = (data_at * tensor_size + tensor_at) * own_count
    own_match = lax.dynamic_slice_in_dim(match_score, first_own, own_count, 0)
    own_level = lax.dynamic_slice_in_dim(level, first_own, own_count, 0)
    own_partner = lax.dynamic_slice_in_dim(partner_units, first_own, own_count, 0)
    unit_grad = (
        unit_grad
        + ((jnp.exp(own_match - own_level) - 1.0) / SOFTMAX_DIVISOR)[:, None] * own_partner
    )
    along = jnp.sum(query_pooled * unit_grad, axis=1, keepdims=True)
    d_pooled = query_inverse * unit_grad - query_pooled * query_inverse**3 * along
    per_token = d_pooled / own_query_lengths.astype(jnp.float32)[:, None]
    d_output = (query_mask[:, :, None] * per_token[:, None, :]).reshape(
        query_result.shape
    ) + token_cotangent.astype(jnp.float32)
    input_gradient, gradients = backward(
        d_output, query_lengths, query_matrices, query_vectors[3], kept
    )
    updated_out = (
        updated[:4]
        + (lax.dynamic_slice_in_dim(updated[4], tensor_at * ff_share, ff_share, 0),)
        + updated[5:]
    )
    return (
        (
            query_result.astype(jnp.bfloat16),
            key_result.astype(jnp.bfloat16),
            contrast_loss,
            input_gradient,
        )
        + gradients
        + updated_out
    )


def solution(mesh):
    in_specs = (
        P(("dp", "tensor"), None),
        P(("dp", "tensor"), None),
        P("dp"),
        P("dp"),
        P(),
        P(("dp", "tensor"), None),
        P(("dp", "tensor"), None),
        P(None, None, "tensor"),
        P(None, "tensor"),
        P("tensor", None),
        P(None, "tensor"),
        P(),
        P("tensor", None),
        P(),
        P(),
        P(),
        P(None, "dp", "tensor"),
        P(None, "tensor"),
        P("tensor", "dp"),
        P("dp", "tensor"),
        P(),
        P("tensor", "dp"),
        P(),
        P(),
        P(),
    )
    out_specs = (
        P(("dp", "tensor"), None),
        P(("dp", "tensor"), None),
        P(),
        P(("dp", "tensor"), None),
        P(None, None, "tensor"),
        P(None, "tensor"),
        P("tensor", None),
        P(None, "tensor"),
        P("tensor"),
        P("tensor", None),
        P(),
        P(),
        P(),
        P(None, "dp", "tensor"),
        P(None, "tensor"),
        P("tensor", "dp"),
        P("dp", "tensor"),
        P("tensor"),
        P("tensor", "dp"),
        P(),
        P(),
        P(),
    )
    return jax.shard_map(local, mesh=mesh, in_specs=in_specs, out_specs=out_specs, check_vma=False)
```

profile of v0, /device:TPU:0, one launch (start us, length us, event | category | flops | bytes accessed | tf_op | source)
XLA Modules:
  0.0 985.1 jit_solution(2148656773947526051)
XLA Ops:
  14.9 33.0 %all_gather.52 = bf16[192,768]{0,1:T(8,128)(2,1)S(1)} all-gather(bf16[192,96]{0,1:T(8,128)(2,1)S(1)} %get-tuple-element.307), channel_id=1, replica_groups=mesh['dp'=8,'tensor'=4] {'dp'}, dimensions={1}, use_global_device_ids=true | all-gather | bytes 331776 | tf_op jit(solution)/shard_map/all_gather | solution.py:323
  48.9 38.0 %all_gather.50 = bf16[3,768,192]{2,0,1:T(4,128)(2,1)S(1)} all-gather(bf16[3,96,192]{2,0,1:T(4,128)(2,1)S(1)} %get-tuple-element.309), channel_id=1, replica_groups=mesh['dp'=8,'tensor'=4] {'dp'}, dimensions={1}, use_global_device_ids=true | all-gather | bytes 995328 | tf_op jit(solution)/shard_map/all_gather | solution.py:322
  87.0 2.9 convolution_bitcast_fusion
  92.7 1.7 fusion.79
  94.4 1.3 fusion.125
  96.8 1.8 convolution_convert_fusion.2
  99.0 2.5 convolution_bitcast_fusion.1
  101.5 1.4 copy-done.17
  104.0 1.7 fusion.123
  106.4 2.1 fusion.124
  111.4 1.8 convolution_convert_fusion.4
  114.6 1.7 fusion.116
  118.4 7.4 reduce-scatter.11.cloned.1.call-done
  128.3 2.0 fusion.77
  131.7 25.5 %reduce-scatter.7.cloned.1.call-done = bf16[256,768]{1,0:T(8,128)(2,1)} async-done(((bf16[1024,768]{1,0:T(8,128)(2,1)}), bf16[256,768]{1,0:T(8,128)(2,1)}) %reduce-scatter.7.cloned.1.call-update) | async-done | bytes 393232 | tf_op jit(solution)/shard_map/reduce_scatter | solution.py:35
  159.7 2.0 fusion.72
  162.6 36.7 %all-gather.22.cloned.1.call-done = bf16[768,768]{1,0:T(8,128)(2,1)} async-done(((bf16[96,768]{1,0:T(8,128)(2,1)}), bf16[768,768]{1,0:T(8,128)(2,1)}) %all-gather.22.cloned.1.call-update) | async-done | bytes 1179664 | tf_op jit(solution)/shard_map/all_gather | solution.py:324
  199.3 20.1 %all-gather.20.cloned.1.call-done = bf16[1024,768]{1,0:T(8,128)(2,1)} async-done(((bf16[256,768]{1,0:T(8,128)(2,1)}), bf16[1024,768]{1,0:T(8,128)(2,1)}) %all-gather.20.cloned.1.call-update) | async-done | bytes 1572880 | tf_op jit(solution)/shard_map/all_gather | solution.py:31
  219.4 6.0 convolution_convert_fusion.1
  225.6 15.5 %all-gather.16.cloned.1.call-done = bf16[1024,768]{1,0:T(8,128)(2,1)} async-done(((bf16[256,768]{1,0:T(8,128)(2,1)}), bf16[1024,768]{1,0:T(8,128)(2,1)}) %all-gather.16.cloned.1.call-update) | async-done | bytes 1572880 | tf_op jit(solution)/shard_map/all_gather | solution.py:31
  241.1 4.9 multiply_convert_fusion.2
  247.2 2.5 convolution_convert_fusion.3
  255.8 16.5 %reduce-scatter.13.cloned.1.call-done = bf16[256,768]{1,0:T(8,128)(2,1)} async-done(((bf16[1024,768]{1,0:T(8,128)(2,1)}), bf16[256,768]{1,0:T(8,128)(2,1)}) %reduce-scatter.13.cloned.1.call-update) | async-done | bytes 393232 | tf_op jit(solution)/shard_map/reduce_scatter | solution.py:35
  272.3 31.4 %reduce-scatter.9.cloned.1.call-done = bf16[256,768]{1,0:T(8,128)(2,1)} async-done(((bf16[1024,768]{1,0:T(8,128)(2,1)}), bf16[256,768]{1,0:T(8,128)(2,1)}) %reduce-scatter.9.cloned.1.call-update) | async-done | bytes 393232 | tf_op jit(solution)/shard_map/reduce_scatter | solution.py:35
  303.7 3.2 fusion.115
  309.6 40.8 %all-gather.3 = bf16[32,1,768]{2,1,0:T(2,128)(2,1)S(1)} all-gather(bf16[1,1,768]{2,1,0:T(2,128)(2,1)S(1)} %convert_bitcast_fusion), channel_id=1, replica_groups=mesh['dp'=8,'tensor'=4] {'dp','tensor'}, dimensions={0}, use_global_device_ids=true | all-gather | bytes 50688 | tf_op jit(solution)/shard_map/all_gather | solution.py:346
  351.0 1.6 fusion.126
  354.5 1.4 dynamic-update-slice
  356.5 1.4 dynamic-update-slice.1
  357.8 37.2 %all-reduce.4 = (f32[1024]{0:T(1024)}, f32[1024]{0:T(1024)}) all-reduce(f32[1024]{0:T(1024)} %dynamic-update-slice, f32[1024]{0:T(1024)} %dynamic-update-slice.1), channel_id=2, replica_groups=mesh['dp'=8,'tensor'=4] {'dp','tensor'}, use_global_device_ids=true, to_apply=%add | all-reduce | flops 2048 | bytes 16384
  396.2 1.4 reshape.377
  398.8 1.4 reshape.376
  401.0 1.7 multiply_reduce_fusion.5
  405.3 40.7 %all-gather.4 = bf16[32,1,768]{2,1,0:T(2,128)(2,1)S(1)} all-gather(bf16[1,1,768]{2,1,0:T(2,128)(2,1)S(1)} %reshape.390), channel_id=4, replica_groups=mesh['dp'=8,'tensor'=4] {'dp','tensor'}, dimensions={0}, use_global_device_ids=true | all-gather | bytes 50688 | tf_op jit(solution)/shard_map/all_gather | solution.py:347
  446.1 38.7 %while.17 = (s32[]{:T(128)}, f32[32]{0:T(128)}, f32[32]{0:T(128)}, f32[32,32]{1,0:T(8,128)}, f32[32,32]{1,0:T(8,128)}, /*index=5*/s32[]{:T(128)}, s32[]{:T(128)}, s32[]{:T(128)}) while((s32[]{:T(128)}, f32[32]{0:T(128)}, f32[32]{0:T(128)}, f32[32,32]{1,0:T(8,128)}, f32[32,32]{1,0:T(8,128)}, /*index=5*/s32[]{:T(128)}, s32[]{:T(128)}, ...), condition=%wide.region_21.22_spmd, body=%wide.region_20.21_spmd.sunk | while | flops 197 | bytes 891 | solution.py:25
  487.9 2.1 fusion.95
  493.5 113.4 %all-reduce.10.cloned.1.call-done = f32[32,768]{1,0:T(8,128)} async-done(((f32[32,768]{1,0:T(8,128)}), f32[32,768]{1,0:T(8,128)}) %all-reduce.10.cloned.1.call-update) | async-done | bytes 98320
  606.8 1.4 multiply_reduce_fusion.15
  608.9 1.8 multiply_reduce_fusion.1
  610.7 2.1 fusion.114
  612.8 20.6 %all-gather.26.cloned.1.call-done = bf16[1024,768]{1,0:T(8,128)(2,1)} async-done(((bf16[256,768]{1,0:T(8,128)(2,1)}), bf16[1024,768]{1,0:T(8,128)(2,1)}) %all-gather.26.cloned.1.call-update) | async-done | bytes 1572880 | tf_op jit(solution)/shard_map/all_gather | solution.py:41
  633.4 5.4 convert_reduce_fusion
  640.0 2.6 convolution_convert_fusion
  642.6 28.3 %reduce-scatter.15.cloned.1.call-done = bf16[256,768]{1,0:T(8,128)(2,1)} async-done(((bf16[1024,768]{1,0:T(8,128)(2,1)}), bf16[256,768]{1,0:T(8,128)(2,1)}) %reduce-scatter.15.cloned.1.call-update) | async-done | bytes 393232 | tf_op jit(solution)/shard_map/reduce_scatter | solution.py:45
  670.9 2.2 multiply_reduce_fusion.2
  673.1 2.0 fusion.113
  676.9 19.5 %all-gather.28.cloned.1.call-done = bf16[1024,768]{1,0:T(8,128)(2,1)} async-done(((bf16[256,768]{1,0:T(8,128)(2,1)}), bf16[1024,768]{1,0:T(8,128)(2,1)}) %all-gather.28.cloned.1.call-update) | async-done | bytes 1572880 | tf_op jit(solution)/shard_map/all_gather | solution.py:41
  696.4 2.1 convolution_convert_fusion.5
  698.8 3.6 fusion.86
  702.4 1.3 fusion.59
  703.8 5.3 fusion.53
  709.0 4.9 fusion.56
  714.0 1.4 copy.137
  718.1 2.6 bitcast_convert_fusion
  721.0 4.9 fusion.129
  725.9 2.8 fusion.128
  730.3 2.3 fusion.39
  735.1 44.6 %all-reduce.3 = (f32[2,768]{1,0:T(2,128)}, f32[2,768]{1,0:T(2,128)}, f32[2,768]{1,0:T(2,128)}) all-reduce(f32[2,768]{1,0:T(2,128)S(1)} %pad_maximum_fusion, f32[2,768]{1,0:T(2,128)S(1)} %pad_maximum_fusion.1, f32[2,768]{1,0:T(2,128)S(1)} %pad_maximum_fusion.2), channel_id=1, replica_groups=mesh['dp'=8,'tensor'=4] {'dp','tensor'}, use_global_device_ids=true, to_apply=%region_45.46 | all-reduce | flops 4608 | bytes 36864 | tf_op jit(solution)/shard_map/psum | solution.py:228
  779.9 23.6 %all-reduce.5 = (f32[2,192]{1,0:T(2,128)}, f32[768]{0:T(1024)}) all-reduce(f32[2,192]{1,0:T(2,128)S(1)} %convert_reduce_fusion.1, f32[768]{0:T(1024)S(1)} %copy-done.75), channel_id=1, replica_groups=mesh['dp'=8,'tensor'=4] {'dp'}, use_global_device_ids=true, to_apply=%region_37.38 | all-reduce | flops 1152 | bytes 9216 | tf_op jit(solution)/shard_map/psum | solution.py:215
  803.6 1.9 convert_add_fusion
  805.5 164.0 %all-reduce.12.cloned.1.call-done = (f32[3,768,192]{1,2,0:T(8,128)}, f32[192,768]{1,0:T(8,128)}, f32[768,768]{1,0:T(8,128)}, f32[768,768]{1,0:T(8,128)}) async-done(((f32[3,768,192]{1,2,0:T(8,128)}, f32[192,768]{1,0:T(8,128)}, f32[768,768]{1,0:T(8,128)}, f32[768,768]{1,0:T(8,128)}), (f32[3,768,192]{1,2,0:T(8,128)}, f32[192,768]{1,0:T(8,128)}, f32[768,768]{1,0:T(8,128)}, ...) | async-done | bytes 7077904 | tf_op jit(solution)/shard_map/psum | solution.py:215
  969.6 2.9 copy.217
  973.3 1.4 copy.219
  975.9 1.4 copy.220
  (362 shorter events, 100.3 us)
Async XLA Ops:
  8.0 105.4 %copy-start = (bf16[768,768]{1,0:T(8,128)(2,1)S(1)}, bf16[768,768]{1,0:T(8,128)(2,1)}, u32[]{:S(2)}) copy-start(bf16[768,768]{1,0:T(8,128)(2,1)} %param.39) | copy-start | bytes 3538948
  8.0 39.8 %copy-start.32 = (f32[3,96,192]{2,1,0:T(8,128)S(1)}, f32[3,96,192]{2,1,0:T(8,128)}, u32[]{:S(2)}) copy-start(f32[3,96,192]{2,1,0:T(8,128)} %param.43) | copy-start | bytes 663556
  8.1 79.0 %all-gather.18.cloned.1.call-start = ((), (), s32[]{:S(2)}) async-start(), calls=%async_computation.10 | async-start | bytes 1966080 | tf_op jit(solution)/shard_map/all_gather | solution.py:31
  8.8 90.2 %all-gather.14.cloned.1.call-start = ((), (), s32[]{:S(2)}) async-start(), calls=%async_computation.6 | async-start | bytes 1966080 | tf_op jit(solution)/shard_map/all_gather | solution.py:31
  9.5 77.4 %copy-start.80 = (s32[4]{0:T(128)S(1)}, s32[4]{0:T(128)}, u32[]{:S(2)}) copy-start(s32[4]{0:T(128)} %param.30) | copy-start | bytes 52
  9.5 116.3 %reduce-scatter.11.cloned.1.call-start = ((), (), s32[]{:S(2)}) async-start(), calls=%async_computation.11 | async-start | bytes 1966080 | tf_op jit(solution)/shard_map/reduce_scatter | solution.py:35
  98.6 58.5 %reduce-scatter.7.cloned.1.call-start = ((), (), s32[]{:S(2)}) async-start(), calls=%async_computation.7 | async-start | bytes 1966080 | tf_op jit(solution)/shard_map/reduce_scatter | solution.py:35
  98.8 10.2 %copy-start.68 = (f32[3,64]{1,0:T(4,128)}, f32[3,64]{1,0:T(4,128)S(1)}, u32[]{:S(2)}) copy-start(f32[3,64]{1,0:T(4,128)S(1)} %add.374) | copy-start | bytes 2308
  98.9 7.5 copy-start.67
  106.0 3.7 copy-start.14
  106.4 3.3 copy-start.13
  113.1 3.3 copy-start.64
  113.1 3.3 copy-start.70
  113.1 4.0 copy-start.63
  113.1 4.0 copy-start.71
  113.2 4.6 copy-start.62
  113.2 4.6 copy-start.72
  113.2 12.6 %copy-start.6 = (bf16[256,768]{1,0:T(8,128)(2,1)S(1)}, bf16[256,768]{1,0:T(8,128)(2,1)}, u32[]{:S(2)}) copy-start(bf16[256,768]{1,0:T(8,128)(2,1)} %param.28) | copy-start | bytes 1179652
  113.2 49.4 %all-gather.24.cloned.1.call-start = ((), (), s32[]{:S(2)}) async-start(), calls=%async_computation.14 | async-start | bytes 1327104 | tf_op jit(solution)/shard_map/all_gather | solution.py:325
  114.5 42.6 %copy-start.4 = (bf16[256,768]{1,0:T(8,128)(2,1)S(1)}, bf16[256,768]{1,0:T(8,128)(2,1)}, u32[]{:S(2)}) copy-start(bf16[256,768]{1,0:T(8,128)(2,1)} %param.27) | copy-start | bytes 1179652
  114.6 84.7 %all-gather.22.cloned.1.call-start = ((), (), s32[]{:S(2)}) async-start(), calls=%async_computation.13 | async-start | bytes 1327104 | tf_op jit(solution)/shard_map/all_gather | solution.py:324
  116.4 103.0 %all-gather.20.cloned.1.call-start = ((), (), s32[]{:S(2)}) async-start(), calls=%async_computation.12 | async-start | bytes 1966080 | tf_op jit(solution)/shard_map/all_gather | solution.py:31
  117.1 42.5 %copy-start.38 = (f32[768]{0:T(1024)}, f32[768]{0:T(1024)S(1)}, u32[]{:S(2)}) copy-start(f32[768]{0:T(1024)S(1)} %get-tuple-element.257) | copy-start | bytes 9220
  117.1 40.0 %copy-start.47 = (f32[2,768]{1,0:T(2,128)}, f32[2,768]{1,0:T(2,128)S(1)}, u32[]{:S(2)}) copy-start(f32[2,768]{1,0:T(2,128)S(1)} %add_multiply_fusion.5) | copy-start | bytes 18436
  117.8 41.9 %copy-start.39 = (f32[768]{0:T(1024)}, f32[768]{0:T(1024)S(1)}, u32[]{:S(2)}) copy-start(f32[768]{0:T(1024)S(1)} %get-tuple-element.255) | copy-start | bytes 9220
  117.8 41.9 %copy-start.48 = (f32[2,768]{1,0:T(2,128)}, f32[2,768]{1,0:T(2,128)S(1)}, u32[]{:S(2)}) copy-start(f32[2,768]{1,0:T(2,128)S(1)} %add_multiply_fusion.6) | copy-start | bytes 18436
  127.0 4.0 copy-start.61
  128.3 33.5 %copy-start.52 = (bf16[3072]{0:T(1024)(128)(2,1)S(1)}, bf16[3072]{0:T(1024)(128)(2,1)}, u32[]{:S(2)}) copy-start(bf16[3072]{0:T(1024)(128)(2,1)} %param.38) | copy-start | bytes 18436
  130.3 110.7 %all-gather.16.cloned.1.call-start = ((), (), s32[]{:S(2)}) async-start(), calls=%async_computation.8 | async-start | bytes 1966080 | tf_op jit(solution)/shard_map/all_gather | solution.py:31
  131.7 93.7 %copy-start.40 = (f32[768]{0:T(1024)}, f32[768]{0:T(1024)S(1)}, u32[]{:S(2)}) copy-start(f32[768]{0:T(1024)S(1)} %get-tuple-element.263) | copy-start | bytes 9220
  158.4 67.0 %copy-start.41 = (f32[256]{0:T(256)}, f32[256]{0:T(256)S(1)}, u32[]{:S(2)}) copy-start(f32[256]{0:T(256)S(1)} %broadcast_multiply_fusion.7) | copy-start | bytes 3076
  159.7 65.7 %copy-start.44 = (f32[256]{0:T(256)}, f32[256]{0:T(256)S(1)}, u32[]{:S(2)}) copy-start(f32[256]{0:T(256)S(1)} %add_rsqrt_fusion.3) | copy-start | bytes 3076
  161.7 110.6 %reduce-scatter.13.cloned.1.call-start = ((), (), s32[]{:S(2)}) async-start(), calls=%async_computation.15 | async-start | bytes 1966080 | tf_op jit(solution)/shard_map/reduce_scatter | solution.py:35
  162.6 62.8 %copy-start.73 = (f32[768]{0:T(1024)}, f32[768]{0:T(1024)S(1)}, u32[]{:S(2)}) copy-start(f32[768]{0:T(1024)S(1)} %fusion.99) | copy-start | bytes 9220
  225.4 78.3 %reduce-scatter.9.cloned.1.call-start = ((), (), s32[]{:S(2)}) async-start(), calls=%async_computation.9 | async-start | bytes 1966080 | tf_op jit(solution)/shard_map/reduce_scatter | solution.py:35
  225.6 20.4 %copy-start.76 = (f32[768]{0:T(1024)}, f32[768]{0:T(1024)S(1)}, u32[]{:S(2)}) copy-start(f32[768]{0:T(1024)S(1)} %dynamic_slice.61) | copy-start | bytes 9220
  247.2 3.2 copy-start.83
  247.2 7.6 copy-start.84
  247.2 56.5 %copy-start.5 = (bf16[256,768]{1,0:T(8,128)(2,1)S(1)}, bf16[256,768]{1,0:T(8,128)(2,1)}, u32[]{:S(2)}) copy-start(bf16[256,768]{1,0:T(8,128)(2,1)} %reduce-scatter.7.cloned.1.call-done) | copy-start | bytes 1179652
  247.2 56.5 %copy-start.10 = (bf16[256,768]{1,0:T(8,128)(2,1)S(1)}, bf16[256,768]{1,0:T(8,128)(2,1)}, u32[]{:S(2)}) copy-start(bf16[256,768]{1,0:T(8,128)(2,1)} %reduce-scatter.11.cloned.1.call-done) | copy-start | bytes 1179652
  249.8 357.1 %all-reduce.10.cloned.1.call-start = ((), (), s32[]{:S(2)}) async-start(), calls=%async_computation.20 | async-start | bytes 196608
  303.7 3.5 copy-start.53
  303.7 3.5 copy-start.65
  307.0 93.8 %copy-start.9 = (f32[256,768]{1,0:T(8,128)S(1)}, f32[256,768]{1,0:T(8,128)}, u32[]{:S(2)}) copy-start(f32[256,768]{1,0:T(8,128)} %get-tuple-element.304) | copy-start | bytes 2359300
  402.7 206.1 %copy-start.21 = (bf16[256,768]{1,0:T(8,128)(2,1)S(1)}, bf16[256,768]{1,0:T(8,128)(2,1)}, u32[]{:S(2)}) copy-start(bf16[256,768]{1,0:T(8,128)(2,1)} %param.33) | copy-start | bytes 1179652
  490.0 143.4 %all-gather.26.cloned.1.call-start = ((), (), s32[]{:S(2)}) async-start(), calls=%async_computation.16 | async-start | bytes 1966080 | tf_op jit(solution)/shard_map/all_gather | solution.py:41
  612.8 58.1 %reduce-scatter.15.cloned.1.call-start = ((), (), s32[]{:S(2)}) async-start(), calls=%async_computation.17 | async-start | bytes 1966080 | tf_op jit(solution)/shard_map/reduce_scatter | solution.py:45
  633.4 6.6 copy-start.51
  640.0 30.9 %copy-start.42 = (f32[256]{0:T(256)S(1)}, f32[256]{0:T(256)}, u32[]{:S(2)}) copy-start(f32[256]{0:T(256)} %copy-done.41) | copy-start | bytes 3076
  640.0 30.9 %copy-start.45 = (f32[256]{0:T(256)S(1)}, f32[256]{0:T(256)}, u32[]{:S(2)}) copy-start(f32[256]{0:T(256)} %copy-done.44) | copy-start | bytes 3076
  642.6 53.8 %all-gather.28.cloned.1.call-start = ((), (), s32[]{:S(2)}) async-start(), calls=%async_computation.18 | async-start | bytes 1966080 | tf_op jit(solution)/shard_map/all_gather | solution.py:41
  673.1 3.8 copy-start.34
  673.1 3.8 copy-start.36
  673.1 23.3 %copy-start.27 = (bf16[192,768]{1,0:T(8,128)(2,1)S(1)}, bf16[192,768]{1,0:T(8,128)(2,1)}, u32[]{:S(2)}) copy-start(bf16[192,768]{1,0:T(8,128)(2,1)} %param.36) | copy-start | bytes 884740
  676.8 126.8 %reduce-scatter.17.cloned.1.call-start = ((), (), s32[]{:S(2)}) async-start(), calls=%async_computation.19 | async-start | bytes 1966080 | tf_op jit(solution)/shard_map/reduce_scatter | solution.py:45
  698.8 3.6 copy-start.3
  703.8 5.3 copy-start.19
  720.7 248.9 %all-reduce.12.cloned.1.call-start = ((), (), s32[]{:S(2)}) async-start(), calls=%async_computation.21 | async-start | bytes 14155776 | tf_op jit(solution)/shard_map/psum | solution.py:215
  721.0 4.9 copy-start.79
  721.0 4.9 copy-start.87
  732.6 47.3 %copy-start.75 = (f32[768]{0:T(1024)S(1)}, f32[768]{0:T(1024)}, u32[]{:S(2)}) copy-start(f32[768]{0:T(1024)} %get-tuple-element.332) | copy-start | bytes 9220
  732.6 71.0 %copy-start.8 = (f32[256,768]{1,0:T(8,128)S(1)}, f32[256,768]{1,0:T(8,128)}, u32[]{:S(2)}) copy-start(f32[256,768]{1,0:T(8,128)} %copy-done.7) | copy-start | bytes 2359300
  969.6 3.8 copy-start.16
  973.3 3.9 copy-start.1
  (40 other events, 72.6 us)
Sparse Core Ops, SparseCore 0:
  10.4 22.3 all-gather.17
  34.4 19.6 all-gather.13
  98.7 27.0 reduce-scatter.10
  128.9 28.1 reduce-scatter.6
  490.1 116.6 all-reduce.9
  612.9 20.4 all-gather.25
  642.7 28.1 reduce-scatter.14
  720.8 28.6 reduce-scatter.16
Sparse Core Ops, SparseCore 1:
  116.4 40.1 all-gather.23
  159.3 40.0 all-gather.21
  201.4 17.9 all-gather.19
  221.5 19.5 all-gather.15
  244.2 28.1 reduce-scatter.12
  275.6 28.0 reduce-scatter.8
  676.9 19.5 all-gather.27
  732.8 236.8 all-reduce.11
where the time goes:
time: 996 us; the launch traced here: 985 us
  waiting for transfers between devices  501 us (50%)
  blocking collectives  258 us (26%)
  other arithmetic  84.6 us (8%)
  matrix products  70.2 us (7%)
  local copies, waits for them, and re-layouts  49.2 us (5%)
  between operations  21.3 us (2%)
    psum x1, waiting for transfers between devices, backward(): lax.psum((grad_heads_in, grad_heads_bias, grad_heads_out, grad_expand, gr...  164 us
    unnamed x17, waiting for transfers between devices  115 us
    reduce_scatter x4, waiting for transfers between devices, sum_rows(): lax.psum_scatter(inputs.astype(jnp.bfloat16), 'tensor', scatter_dimension...  80.8 us
    psum x1, blocking collectives, backward(): lax.psum((bias_pair, jnp.stack([gain_one, gain_two]), jnp.stack([shift_on...  44.6 us
    all_gather x1, blocking collectives, local(): lax.all_gather(query_unit.astype(jnp.bfloat16), ('dp', 'tensor'), axis=0,...  40.8 us
    all_gather x1, blocking collectives, local(): lax.all_gather(key_unit.astype(jnp.bfloat16), ('dp', 'tensor'), axis=0, t...  40.7 us
    all_gather x2, waiting for transfers between devices, gather_grads(): return lax.all_gather(inputs, 'tensor', axis=0, tiled=True)  40.1 us
    add x31, other arithmetic, merge_stats(): first[1] * jnp.exp(first[0] - peak) + second[1] * jnp.exp(second[0] - peak)  38.7 us
  transfers between devices with their start and end apart: 16, of which 12 were waited for; matrix products, arithmetic and copies ran while one was open for 8% of the time, Pallas kernels for 0%

commit v1 on v0

v1 whole, which is shorter than its diff:
```python
import types

import jax
import jax.numpy as jnp
from jax import lax
from jax.experimental import pallas as pl
from jax.experimental.pallas import tpu as pltpu
from jax.sharding import PartitionSpec as P

HEAD = 64
SOFTMAX_DIVISOR = 0.05
MOMENTUM = 0.5
NORM_EPSILON = 1e-12
MASKED_SCORE = -1e30
ROOT_HALF = 0.7071067811865476
GAUSS_SCALE = 0.3989422804014327
MESH = pl.DeviceIdType.MESH
F32, BF16 = jnp.float32, jnp.bfloat16
NN = (((1,), (0,)), ((), ()))
NT = (((1,), (1,)), ((), ()))
TN = (((0,), (0,)), ((), ()))
TENSOR = 4
PIECES = 6


def dot(a, b, dims=NN):
    return lax.dot_general(a, b, dims, preferred_element_type=F32)


def norm_rows(v, gain, shift):
    c = v - jnp.mean(v, axis=-1, keepdims=True)
    inverse = lax.rsqrt(jnp.mean(c * c, axis=-1, keepdims=True) + NORM_EPSILON)
    n = c * inverse
    return n * gain + shift, n, inverse


def norm_back(up, n, inverse, gain):
    e = up * gain
    inner = e - jnp.mean(e, axis=-1, keepdims=True) - n * jnp.mean(e * n, axis=-1, keepdims=True)
    return inner * inverse


def gelu_parts(z):
    a = jnp.abs(z) * ROOT_HALF
    g = jnp.exp(-0.5 * z * z)
    s = 1.0 / (1.0 + 0.3275911 * a)
    poly = ((((1.061405429 * s - 1.453152027) * s + 1.421413741) * s - 0.284496736) * s + 0.254829592) * s
    q = 0.5 * poly * g
    cdf = jnp.where(z >= 0, 1.0 - q, q)
    return z * cdf, cdf + z * GAUSS_SCALE * g


def kernel(cfg, *refs):
    r = types.SimpleNamespace(**dict(zip(cfg.names, refs)))
    D, HS, FS, L, DP, RC = cfg.D, cfg.HS, cfg.FS, cfg.L, cfg.DP, cfg.RC
    N, SH, NZ = DP * TENSOR, cfg.SH, DP // 2
    NCH = L // RC
    dp, t = lax.axis_index("dp"), lax.axis_index("tensor")
    px = lax.rem(t + 2, TENSOR)
    sib = t + 1 - 2 * lax.rem(t, 2)
    y, z = lax.rem(dp, 2), dp // 2
    me = dp * TENSOR + t
    d_x, d_sib, d_y = (dp, px), (dp, sib), (dp + 1 - 2 * y, t)

    def d_z(k):
        return (lax.rem(z + k, NZ) * 2 + y, t)

    def from_z(k):
        return lax.rem(z - k + NZ, NZ)

    def remote(src, dst, sems, i, dev):
        return pltpu.make_async_remote_copy(
            src_ref=src, dst_ref=dst, send_sem=sems[0].at[i], recv_sem=sems[1].at[i], device_id=dev, device_id_type=MESH
        )

    sends = []

    def send(src, dst, sems, i, dev):
        c = remote(src, dst, sems, i, dev)
        c.start()
        sends.append(c)
        return c

    loads = {}

    def load(name, src, dst):
        c = pltpu.make_async_copy(src, dst, r.lsem.at[len(loads)])
        c.start()
        loads[name] = c

    stores = []

    def store(src, dst):
        c = pltpu.make_async_copy(src, dst, r.ssem.at[len(stores)])
        c.start()
        stores.append(c)

    xs, cs = (r.xs, r.xr), (r.cs, r.cr)

    load("q", r.query_tokens, r.X.at[0, 0])
    load("hi", r.heads_in, r.wqi.at[0])
    load("mhi", r.momentum_heads_in, r.mhi) if cfg.gather else None
    load("we", r.expand_weight, r.we.at[0])
    load("wo", r.heads_out, r.wo.at[0])
    load("ws", r.shrink_weight, r.ws.at[0])
    if cfg.gather:
        load("me", r.momentum_expand_weight, r.mex)
        load("mo", r.momentum_heads_out, r.mho)
        load("ms", r.momentum_shrink_weight, r.msh)
    else:
        load("kh", r.key_heads, r.wkh.at[0])
        load("kf", r.key_ffn, r.wkf.at[0])
    load("k", r.key_tokens, r.X.at[1, 0])
    load("queue", r.key_queue, r.queue)
    load("cot", r.token_cotangent, r.cot)

    bar = pltpu.get_barrier_semaphore()

    def greet(i, c):
        o = lax.rem(me + i, N)
        pl.semaphore_signal(bar, inc=1, device_id=(o // TENSOR, lax.rem(o, TENSOR)), device_id_type=MESH)
        return c

    lax.fori_loop(1, N, greet, 0)
    pl.semaphore_wait(bar, N - 1)

    c_xq = send(r.query_tokens, r.X.at[0, 1], xs, 0, d_x)
    c_hi = send(r.heads_in, r.wqi.at[1], cs, 0, d_sib)
    c_wo = send(r.heads_out, r.wo.at[1], cs, 1, d_sib)
    c_we = send(r.expand_weight, r.we.at[1], cs, 2, d_sib)
    c_ws = send(r.shrink_weight, r.ws.at[1], cs, 3, d_sib)
    c_xk = send(r.key_tokens, r.X.at[1, 1], xs, 1, d_x)

    def vec(ref, k):
        return ref[...].astype(F32)[k : k + 1, :]

    def blend_vec(old, new):
        return MOMENTUM * old[...] + (1.0 - MOMENTUM) * new[...].astype(F32)

    r.hb[0, 0:2, :] = r.heads_bias[...].astype(F32)
    r.hb[0, 2:4, :] = blend_vec(r.momentum_heads_bias, r.heads_bias)
    c_hb = send(r.hb.at[0], r.hb.at[1], cs, 4, d_sib)
    kbb = blend_vec(r.momentum_branch_bias, r.branch_bias)
    kgain = blend_vec(r.momentum_norm_gain, r.norm_gain)
    kshift = blend_vec(r.momentum_norm_shift, r.norm_shift)
    bb = (r.branch_bias[...].astype(F32), kbb)
    gain = (r.norm_gain[...].astype(F32), kgain)
    shift = (r.norm_shift[...].astype(F32), kshift)
    r.eb[0] = r.expand_bias[...].astype(F32)
    r.eb[1] = MOMENTUM * r.momentum_expand_bias[...] + (1.0 - MOMENTUM) * r.expand_bias[...].astype(F32)

    gs = (r.gs, r.gr)
    gy0, gc0 = 2 * (NZ - 1), 2 * (NZ - 1) + 2 * NZ
    gparts = ((r.wkh, 4), (r.wkf, 2))

    def g_rows(part, owner):
        return gparts[part][0].at[0, :, pl.ds(pl.multiple_of(owner * SH, SH), SH), :]

    gz, gy = {}, {}

    def g_start(part):
        for k in range(1, NZ):
            gz[part, k] = send(g_rows(part, dp), g_rows(part, dp), gs, part * (NZ - 1) + k - 1, d_z(k))
        gy[part, 0] = send(g_rows(part, dp), g_rows(part, dp), gs, gy0 + part * NZ, d_y)

    def g_forward(part):
        for k in range(1, NZ):
            gz[part, k].wait_recv()
            rows = g_rows(part, from_z(k) * 2 + y)
            gy[part, k] = send(rows, rows, gs, gy0 + part * NZ + k, d_y)

    g_done = {}

    def g_finish(part):
        for k in range(NZ):
            gy[part, k].wait_recv()
        buf = gparts[part][0]
        g_done[part] = send(buf.at[0], buf.at[1], gs, gc0 + part, d_sib)

    if cfg.gather:
        own = pl.ds(pl.multiple_of(dp * SH, SH), SH)
        pick = (
            lax.broadcasted_iota(jnp.int32, (D, SH), 0) == lax.broadcasted_iota(jnp.int32, (D, SH), 1) + dp * SH
        ).astype(F32).astype(BF16)
        eye = (
            lax.broadcasted_iota(jnp.int32, (SH, SH), 0) == lax.broadcasted_iota(jnp.int32, (SH, SH), 1)
        ).astype(F32).astype(BF16)
        for name in ("hi", "mhi", "wo", "mo"):
            loads[name].wait()
        for i in range(3):
            u = MOMENTUM * r.mhi[i] + (1.0 - MOMENTUM) * r.wqi[0, i, own, :].astype(F32)
            r.mhi[i] = u
            r.wkh[0, i, own, :] = u.astype(BF16)
        u = MOMENTUM * r.mho[...] + (1.0 - MOMENTUM) * dot(r.wo[0], pick)
        r.mho[...] = u
        r.wkh[0, 3, own, :] = dot(eye, u.astype(BF16), NT).astype(BF16)
        g_start(0)
        for name in ("we", "me", "ws", "ms"):
            loads[name].wait()
        u = MOMENTUM * r.mex[...] + (1.0 - MOMENTUM) * r.we[0, own, :].astype(F32)
        r.mex[...] = u
        r.wkf[0, 0, own, :] = u.astype(BF16)
        u = MOMENTUM * r.msh[...] + (1.0 - MOMENTUM) * dot(r.ws[0], pick)
        r.msh[...] = u
        r.wkf[0, 1, own, :] = dot(eye, u.astype(BF16), NT).astype(BF16)
        g_start(1)
        store(r.mhi, r.o_heads_in)
        store(r.mho, r.o_heads_out)
        store(r.mex, r.o_expand)
        store(r.msh, r.o_shrink)
    else:
        for name in ("hi", "wo", "we", "ws", "kh", "kf"):
            loads[name].wait()
        for part in range(2):
            buf = gparts[part][0]
            g_done[part] = send(buf.at[0], buf.at[1], gs, gc0 + part, d_sib)

    lengths = ((r.query_lengths[t], r.query_lengths[px]), (r.key_lengths[t], r.key_lengths[px]))
    low_half = lax.broadcasted_iota(jnp.int32, (1, 128), 1) < HEAD
    key_at = lax.broadcasted_iota(jnp.int32, (1, L), 1)

    def heads_of(arr):
        pair, last = arr[:, 0:128], arr[:, 128:192]
        zero = jnp.zeros_like(pair)
        return (jnp.where(low_half, pair, zero), jnp.where(low_half, zero, pair), last)

    def attend(w, crop, out):
        x = r.X[w, crop]
        valid = key_at < lengths[w][crop]

        def slot_step(s, c):
            if w == 0:
                wq, wk, wv = r.wqi[s, 0], r.wqi[s, 1], r.wqi[s, 2]
            else:
                wq, wk, wv = r.wkh[s, 0], r.wkh[s, 1], r.wkh[s, 2]
            hb = r.hb[s]
            q = ((dot(x, wq) + hb[2 * w : 2 * w + 1, :]).astype(BF16).astype(F32) * HEAD**-0.5).astype(BF16)
            k = dot(x, wk).astype(BF16)
            v = (dot(x, wv) + hb[2 * w + 1 : 2 * w + 2, :]).astype(BF16)
            if w == 0:
                r.qkv[s, 0, crop], r.qkv[s, 1, crop], r.qkv[s, 2, crop] = q, k, v
            ks, vs, qs = heads_of(k), heads_of(v), (q[:, 0:128], q[:, 0:128], q[:, 128:192])
            parts, logs = [], []
            for h in range(3):
                sc = jnp.where(valid, dot(qs[h], ks[h], NT), MASKED_SCORE)
                top = jnp.max(sc, axis=-1, keepdims=True)
                e = jnp.exp(sc - top)
                tot = jnp.sum(e, axis=-1, keepdims=True)
                logs.append(top + jnp.log(tot))
                parts.append(dot((e * (1.0 / tot)).astype(BF16), vs[h]))
            c01 = (parts[0] + parts[1]).astype(BF16)
            c2 = parts[2].astype(BF16)
            ctx = jnp.concatenate([c01, c2], axis=1)
            if w == 0:
                at = lax.broadcasted_iota(jnp.int32, (L, 128), 1)
                r.G[s, crop] = jnp.where(at == 0, logs[0], jnp.where(at == 1, logs[1], logs[2]))
                r.C[s, crop] = ctx
                a = dot(ctx, r.wo[s])
            else:
                a = dot(ctx, r.wkh[s, 3], NT)

            @pl.when(s == 0)
            def _():
                out[...] = a

            @pl.when(s != 0)
            def _():
                out[...] += a

            return c

        lax.fori_loop(0, 2, slot_step, 0)

    def swap(src32, sbuf, rbuf, base):
        out = []
        for j in range(NCH):
            rows = pl.ds(j * RC, RC)
            sbuf[rows, :] = src32[rows, :].astype(BF16)
            out.append(send(sbuf.at[rows], rbuf.at[rows], xs, base + j, d_x))
        return out

    FT = 256

    def feed(w, crop, row0, rows_n, out):
        rows = pl.ds(row0, rows_n)
        u = r.U[w, crop, rows, :]

        def step(i, c):
            s, j = i // (FS // FT), lax.rem(i, FS // FT)
            cols = pl.ds(pl.multiple_of(j * FT, FT), FT)
            at = jnp.where(s == 0, t, sib)
            b = r.eb[w, pl.ds(at, 1), cols]
            if w == 0:
                zz = dot(u, r.we[s, :, cols]) + b
            else:
                zz = dot(u, r.wkf[s, 0, :, cols]) + b
            h, slope = gelu_parts(zz)
            h = h.astype(BF16)
            if w == 0:
                r.H[s, crop, rows, cols] = h
                r.slope[s, crop, rows, cols] = slope.astype(BF16)
                f = dot(h, r.ws[s, cols, :])
            else:
                f = dot(h, r.wkf[s, 1, :, cols], NT)

            @pl.when(i == 0)
            def _():
                out[rows, :] = f

            @pl.when(i != 0)
            def _():
                out[rows, :] += f

            return c

        lax.fori_loop(0, 2 * (FS // FT), step, 0)

    x_of = {}

    def first_norm(w, base):
        out = []
        for j in range(NCH):
            rows = pl.ds(j * RC, RC)
            x_of["A", w][j].wait_recv()
            m = r.X[w, 0, rows, :].astype(F32) + (r.own[w, rows, :] + r.arecv[w, rows, :].astype(F32)) + bb[w][0:1, :]
            u, n, inv = norm_rows(m, gain[w][0:1, :], shift[w][0:1, :])
            r.Uf[w, rows, :] = u
            r.U[w, 0, rows, :] = u.astype(BF16)
            if w == 0:
                r.N1[rows, :] = n
                r.i1[rows, :] = jnp.broadcast_to(inv, (RC, 128))
            out.append(send(r.U.at[w, 0, rows], r.U.at[w, 1, rows], xs, base + j, d_x))
        x_of["U", w] = out

    def second_norm(w, o_ref, o_hbm):
        pooled = jnp.zeros((1, D), F32)
        length = lengths[w][0]
        for j in range(NCH):
            rows = pl.ds(j * RC, RC)
            x_of["F", w][j].wait_recv()
            m = r.Uf[w, rows, :] + (r.own[w, rows, :] + r.frecv[w, rows, :].astype(F32)) + bb[w][1:2, :]
            out, n, inv = norm_rows(m, gain[w][1:2, :], shift[w][1:2, :])
            o_ref[rows, :] = out.astype(BF16)
            if w == 0:
                r.N2[rows, :] = n
                r.i2[rows, :] = jnp.broadcast_to(inv, (RC, 128))
            valid = lax.broadcasted_iota(jnp.int32, (RC, 1), 0) + j * RC < length
            pooled += jnp.sum(jnp.where(valid, out, 0.0), axis=0, keepdims=True)
        store(o_ref, o_hbm)
        pooled = pooled / length.astype(F32)
        inverse = lax.rsqrt(jnp.sum(pooled * pooled, axis=-1, keepdims=True) + 1e-06)
        unit = (pooled * inverse).astype(BF16).astype(F32)
        return pooled, inverse, unit

    KL = D // 128

    def tile_of(row):
        return jnp.concatenate([row[:, i * 128 : (i + 1) * 128] for i in range(KL)], axis=0)

    def to_all(sbuf_of, rbuf, sems, base):
        def go(i, c):
            o = lax.rem(me + i, N)
            remote(sbuf_of(o), rbuf.at[me], sems, base + i - 1, (o // TENSOR, lax.rem(o, TENSOR))).start()
            return c

        lax.fori_loop(1, N, go, 0)

    def from_all(rbuf, sems, base):
        def go(i, c):
            o = lax.rem(me - i + N, N)
            remote(rbuf.at[o], rbuf.at[o], sems, base + i - 1, d_x).wait_recv()
            return c

        lax.fori_loop(1, N, go, 0)

    def sent_all(sbuf, sems, base):
        def go(i, c):
            remote(sbuf.at[0], sbuf.at[0], sems, base + i - 1, d_x).wait_send()
            return c

        lax.fori_loop(1, N, go, 0)

    us = (r.us, r.ur)

    loads["q"].wait()
    c_hi.wait_recv()
    c_wo.wait_recv()
    c_hb.wait_recv()
    attend(0, 0, r.own.at[0])
    c_xq.wait_recv()
    attend(0, 1, r.part)
    x_of["A", 0] = swap(r.part, r.asend.at[0], r.arecv.at[0], 2)
    if cfg.gather:
        g_forward(0)
    c_we.wait_recv()
    c_ws.wait_recv()
    first_norm(0, 2 + NCH)
    feed(0, 0, 0, L, r.own.at[0])
    if cfg.gather:
        g_finish(0)
    for j in range(NCH):
        x_of["U", 0][j].wait_recv()
        feed(0, 1, j * RC, RC, r.part)
        if j == 0:
            x_of["F", 0] = []
        rows = pl.ds(j * RC, RC)
        r.fsend[0, rows, :] = r.part[rows, :].astype(BF16)
        x_of["F", 0].append(send(r.fsend.at[0, rows], r.frecv.at[0, rows], xs, 2 + 2 * NCH + j, d_x))
    kb = 2 + 3 * NCH
    c_xk.wait_recv()
    loads["k"].wait()
    g_done[0].wait_recv()
    attend(1, 1, r.part)
    x_of["A", 1] = swap(r.part, r.asend.at[1], r.arecv.at[1], kb)
    if cfg.gather:
        g_forward(1)
    attend(1, 0, r.own.at[1])
    q_pooled, q_inverse, q_unit = second_norm(0, r.oq, r.query_output)
    r.usend[0, 0:KL, :] = tile_of(q_unit)
    r.units[0, me, 0:KL, :] = tile_of(q_unit)
    to_all(lambda o: r.usend.at[0], r.units.at[0], us, 0)
    first_norm(1, kb + NCH)
    if cfg.gather:
        g_finish(1)
    g_done[1].wait_recv()
    feed(1, 0, 0, L, r.own.at[1])
    for j in range(NCH):
        x_of["U", 1][j].wait_recv()
        feed(1, 1, j * RC, RC, r.part)
        if j == 0:
            x_of["F", 1] = []
        rows = pl.ds(j * RC, RC)
        r.fsend[1, rows, :] = r.part[rows, :].astype(BF16)
        x_of["F", 1].append(send(r.fsend.at[1, rows], r.frecv.at[1, rows], xs, kb + 2 * NCH + j, d_x))
    loads["queue"].wait()
    from_all(r.units.at[0], us, 0)
    all_q = jnp.concatenate([r.units[0, :, i, :] for i in range(KL)], axis=1).astype(BF16)
    logits = dot(all_q, r.queue[...], NT) / SOFTMAX_DIVISOR
    top = jnp.max(logits, axis=-1, keepdims=True)
    e = jnp.exp(logits - top)
    tot = jnp.sum(e, axis=-1, keepdims=True)
    grad = dot(e.astype(BF16), r.queue[...])
    for i in range(KL):
        r.nsend[:, i, :] = grad[:, i * 128 : (i + 1) * 128]
    r.nsend[:, KL, :] = jnp.broadcast_to(top, (N, 128))
    r.nsend[:, KL + 1, :] = jnp.broadcast_to(tot, (N, 128))
    r.nrecv[me] = r.nsend[me]
    to_all(lambda o: r.nsend.at[o], r.nrecv, us, N - 1)
    k_pooled, k_inverse, k_unit = second_norm(1, r.ok, r.key_output)
    r.usend[1, 0:KL, :] = tile_of(k_unit)
    r.units[1, me, 0:KL, :] = tile_of(k_unit)
    to_all(lambda o: r.usend.at[1], r.units.at[1], us, 2 * (N - 1))
    from_all(r.nrecv, us, N - 1)
    from_all(r.units.at[1], us, 2 * (N - 1))

    pos = r.positives[me]
    hit = lax.broadcasted_iota(jnp.int32, (N, 1, 1), 0) == pos
    partner = jnp.sum(jnp.where(hit, r.units[1][:, 0:KL, :], 0.0), axis=0)
    mine = r.usend[0, 0:KL, :]
    match = jnp.sum(jnp.sum(mine * partner, axis=1, keepdims=True), axis=0, keepdims=True) / SOFTMAX_DIVISOR
    tops, tots = r.nrecv[:, KL, :], r.nrecv[:, KL + 1, :]
    peak = jnp.maximum(jnp.max(jnp.max(tops, axis=0, keepdims=True), axis=1, keepdims=True), match)
    total = jnp.sum(tots * jnp.exp(tops - peak), axis=0, keepdims=True)[:, 0:1]
    level = peak + jnp.log(total + jnp.exp(match - peak))
    loss = level - match
    scale = jnp.exp(r.nrecv[:, KL : KL + 1, :] - level.reshape(1, 1, 1)) * (1.0 / SOFTMAX_DIVISOR)
    du = jnp.sum(r.nrecv[:, 0:KL, :] * scale, axis=0) + (jnp.exp(match - level) - 1.0) / SOFTMAX_DIVISOR * partner
    du = jnp.concatenate([du[i : i + 1, :] for i in range(KL)], axis=1)
    along = jnp.sum(q_pooled * du, axis=-1, keepdims=True)
    d_pooled = q_inverse * du - q_pooled * (q_inverse * q_inverse * q_inverse) * along
    per_token = d_pooled / lengths[0][0].astype(F32)

    loads["cot"].wait()
    bbase = kb + 3 * NCH
    small = [jnp.zeros((1, D), F32) for _ in range(6)]
    x_of["dF"] = []
    for j in range(NCH):
        rows = pl.ds(j * RC, RC)
        valid = lax.broadcasted_iota(jnp.int32, (RC, 1), 0) + j * RC < lengths[0][0]
        dy = r.cot[rows, :].astype(F32) + jnp.where(valid, per_token, 0.0)
        n2 = r.N2[rows, :]
        d2 = norm_back(dy, n2, r.i2[rows, 0:1], gain[0][1:2, :])
        r.d2[rows, :] = d2
        r.dF[0, rows, :] = d2.astype(BF16)
        x_of["dF"].append(send(r.dF.at[0, rows], r.dF.at[1, rows], xs, bbase + j, d_x))
        small[1] += jnp.sum(d2, axis=0, keepdims=True)
        small[3] += jnp.sum(dy * n2, axis=0, keepdims=True)
        small[5] += jnp.sum(dy, axis=0, keepdims=True)

    def feed_back(crop, row0, rows_n, out):
        rows = pl.ds(row0, rows_n)
        df = r.dF[crop, rows, :]

        def step(i, c):
            s, j = i // (FS // FT), lax.rem(i, FS // FT)
            cols = pl.ds(pl.multiple_of(j * FT, FT), FT)
            dh = dot(df, r.ws[s, cols, :], NT)
            dz = (dh * r.slope[s, crop, rows, cols].astype(F32)).astype(BF16)
            r.dZ[s, crop, rows, cols] = dz
            du_ = dot(dz, r.we[s, :, cols], NT)

            @pl.when(i == 0)
            def _():
                out[rows, :] = du_

            @pl.when(i != 0)
            def _():
                out[rows, :] += du_

            return c

        lax.fori_loop(0, 2 * (FS // FT), step, 0)

    feed_back(0, 0, L, r.own.at[0])
    x_of["dU"] = []
    for j in range(NCH):
        x_of["dF"][j].wait_recv()
        feed_back(1, j * RC, RC, r.part)
        rows = pl.ds(j * RC, RC)
        r.dusend[rows, :] = r.part[rows, :].astype(BF16)
        x_of["dU"].append(send(r.dusend.at[rows], r.durecv.at[rows], xs, bbase + NCH + j, d_x))

    PR = 3 * 2 * D // (2 * 3) // 2
    HF, CH = PR // 2, PR // 2 // max(NZ, 1)
    ws_sem = (r.ws_s, r.ws_r)
    per = 2 + 2 * (NZ - 1) + NZ

    def piece_part(p, s, q):
        if p < 2:
            cols = pl.ds(p * PR + q * HF, HF) if (p * PR + q * HF) % 128 == 0 else None
            h = r.H[s].reshape(2 * L, FS)
            h = h[:, p * PR + q * HF : p * PR + (q + 1) * HF]
            return dot(h, r.dF[...].reshape(2 * L, D), TN)
        if p < 4:
            u = r.U[0].reshape(2 * L, D)[:, (p - 2) * PR + q * HF : (p - 2) * PR + (q + 1) * HF]
            return dot(u, r.dZ[s].reshape(2 * L, FS), TN)
        i = (p - 4) * 2 + q
        if i < 3:
            return dot(r.dqkv[s, i].reshape(2 * L, HS), r.X[0].reshape(2 * L, D), TN)
        return dot(r.C[s].reshape(2 * L, HS), r.dA[...].reshape(2 * L, D), TN)

    w_of = {}

    def w_sib(p):
        for q in range(2):
            r.wsend[p, q * HF : (q + 1) * HF, :] = piece_part(p, 1, q).astype(BF16)
        w_of["s", p] = send(r.wsend.at[p], r.wrecv.at[p], ws_sem, p * per, d_sib)

    def half(h):
        return pl.ds(pl.multiple_of(h * HF, HF), HF)

    def w_own(p):
        w_of["s", p].wait_recv()
        for q in range(2):
            rows = slice(q * HF, (q + 1) * HF)
            v = piece_part(p, 0, q) + r.wrecv[p, rows, :].astype(F32)
            if cfg.gather:
                r.wacc[p, rows, :] = v.astype(BF16)
            else:
                r.wacc32[p, rows, :] = v
        if cfg.gather:
            w_of["y", p] = send(r.wacc.at[p, half(1 - y)], r.wyr.at[p], ws_sem, p * per + 1, d_y)
        else:
            store(r.wacc32.at[p], r.grads.at[p])

    def chunk(zz):
        return pl.ds(pl.multiple_of(zz * CH, CH), CH)

    def place(yy, zz):
        return pl.ds(pl.multiple_of(yy * HF + zz * CH, CH), CH)

    def w_y(p):
        w_of["y", p].wait_recv()
        r.wys[p] = (r.wacc[p, half(y), :].astype(F32) + r.wyr[p].astype(F32)).astype(BF16)
        for k in range(1, NZ):
            to = lax.rem(z + k, NZ)
            w_of["z", p, k] = send(r.wys.at[p, chunk(to)], r.wzr.at[p, k - 1], ws_sem, p * per + 1 + k, d_z(k))

    def w_z(p):
        v = r.wys[p, chunk(z), :].astype(F32)
        for k in range(1, NZ):
            w_of["z", p, k].wait_recv()
            v += r.wzr[p, k - 1].astype(F32)
        at = place(y, z)
        r.wout[p, at, :] = v.astype(BF16)
        for k in range(1, NZ):
            w_of["a", p, k] = send(r.wout.at[p, at], r.wout.at[p, at], ws_sem, p * per + NZ + k, d_z(k))
        w_of["b", p, 0] = send(r.wout.at[p, at], r.wout.at[p, at], ws_sem, p * per + 2 * NZ, d_y)

    def w_a(p):
        for k in range(1, NZ):
            w_of["a", p, k].wait_recv()
            at = place(y, from_z(k))
            w_of["b", p, k] = send(r.wout.at[p, at], r.wout.at[p, at], ws_sem, p * per + 2 * NZ + k, d_y)

    def w_b(p):
        for k in range(NZ):
            w_of["b", p, k].wait_recv()
        store(r.wout.at[p], r.grads.at[p])

    if not cfg.gather:
        w_y = w_z = w_a = w_b = lambda p: None

    for p in range(4):
        w_sib(p)
    for p in range(4):
        w_own(p)

    x_of["dA"] = []
    for j in range(NCH):
        rows = pl.ds(j * RC, RC)
        x_of["dU"][j].wait_recv()
        du1 = r.d2[rows, :] + (r.own[0, rows, :] + r.durecv[rows, :].astype(F32))
        n1 = r.N1[rows, :]
        dm = norm_back(du1, n1, r.i1[rows, 0:1], gain[0][0:1, :])
        r.Uf[0, rows, :] = dm
        r.dA[0, rows, :] = dm.astype(BF16)
        x_of["dA"].append(send(r.dA.at[0, rows], r.dA.at[1, rows], xs, bbase + 2 * NCH + j, d_x))
        small[0] += jnp.sum(dm, axis=0, keepdims=True)
        small[2] += jnp.sum(du1 * n1, axis=0, keepdims=True)
        small[4] += jnp.sum(du1, axis=0, keepdims=True)
    for i in range(6):
        r.sm[0, i : i + 1, :] = small[i]
    r.sm[0, 6:7, :] = jnp.broadcast_to(loss, (1, D))
    w_y(0)

    def attend_back(crop, out):
        valid = key_at < lengths[0][crop]

        def slot_step(s, c):
            dc = dot(r.dA[crop], r.wo[s], NT).astype(BF16)
            q, k, v = r.qkv[s, 0, crop], r.qkv[s, 1, crop], r.qkv[s, 2, crop]
            g = r.G[s, crop]
            dcs, qs, ks, vs = heads_of(dc), heads_of(q), heads_of(k), heads_of(v)
            plain = lambda a, h: a[:, 128:192] if h == 2 else a[:, 0:128]
            dq, dk, dv = [], [], []
            for h in range(3):
                sc = jnp.where(valid, dot(plain(q, h), ks[h], NT), MASKED_SCORE)
                pw = jnp.exp(sc - g[:, h : h + 1])
                dpw = dot(plain(dc, h), vs[h], NT)
                inner = jnp.sum(dpw * pw, axis=-1, keepdims=True)
                ds = (pw * (dpw - inner)).astype(BF16)
                dq.append(dot(ds, ks[h]))
                dk.append(dot(ds, qs[h], TN))
                dv.append(dot(pw.astype(BF16), dcs[h], TN))
            join = lambda a, m: jnp.concatenate([((a[0] + a[1]) * m).astype(BF16), (a[2] * m).astype(BF16)], axis=1)
            dq, dk, dv = join(dq, HEAD**-0.5), join(dk, 1.0), join(dv, 1.0)
            r.dqkv[s, 0, crop], r.dqkv[s, 1, crop], r.dqkv[s, 2, crop] = dq, dk, dv
            dx = dot(dq, r.wqi[s, 0], NT) + dot(dk, r.wqi[s, 1], NT) + dot(dv, r.wqi[s, 2], NT)

            @pl.when(s == 0)
            def _():
                out[...] = dx

            @pl.when(s != 0)
            def _():
                out[...] += dx

            return c

        lax.fori_loop(0, 2, slot_step, 0)

    attend_back(0, r.own.at[1])
    w_y(1)
    w_z(0)
    for j in range(NCH):
        x_of["dA"][j].wait_recv()
    attend_back(1, r.part)
    x_of["dX"] = swap(r.part, r.dxsend, r.dxrecv, bbase + 3 * NCH)
    w_sib(4)
    w_sib(5)

    for s in range(2):
        eb = jnp.sum(r.dZ[s].reshape(2 * L, FS).astype(F32), axis=0, keepdims=True)
        bq = jnp.sum(r.dqkv[s, 0].reshape(2 * L, HS).astype(F32), axis=0, keepdims=True)
        bv = jnp.sum(r.dqkv[s, 2].reshape(2 * L, HS).astype(F32), axis=0, keepdims=True)
        dst = r.sm if s == 0 else r.smx
        at = 8 if s == 0 else 0
        if s == 0:
            r.sm[0, 8:9, 0:FS] = eb
            r.sm[0, 9:10, 0:HS] = bq
            r.sm[0, 10:11, 0:HS] = bv
        else:
            r.smx[0:8, :] = r.sm[0, 0:8, :]
            r.smx[8:9, 0:FS] = eb
            r.smx[9:10, 0:HS] = bq
            r.smx[10:11, 0:HS] = bv
    bs = (r.bs, r.br)
    send(r.smx, r.smr.at[0], bs, 0, d_sib).wait_recv()
    r.sm[1] = r.sm[0] + r.smr[0]
    b_x = send(r.sm.at[1, 0:8], r.smr.at[1, 0:8], bs, 1, d_x)
    w_own(4)
    w_own(5)
    w_y(2)
    w_z(1)
    b_x.wait_recv()
    r.sm[2] = r.sm[1]
    r.sm[2, 0:8, :] = r.sm[1, 0:8, :] + r.smr[1, 0:8, :]
    nb = DP.bit_length() - 1 if cfg.gather else 0

    def butterfly(k):
        other = dp + (1 - 2 * lax.rem(dp // (1 << k), 2)) * (1 << k)
        return send(r.sm.at[2 + k], r.smr.at[2 + k], bs, 2 + k, (other, t))

    def add_up(k, c):
        c.wait_recv()
        r.sm[3 + k] = r.sm[2 + k] + r.smr[2 + k]

    b_k = butterfly(0) if nb else None
    for j in range(NCH):
        rows = pl.ds(j * RC, RC)
        x_of["dX"][j].wait_recv()
        r.Uf[1, rows, :] = r.Uf[0, rows, :] + (r.own[1, rows, :] + r.dxrecv[rows, :].astype(F32))
    store(r.Uf.at[1], r.input_gradient)
    order = [(w_y, 3), (w_z, 2), (w_a, 0), (w_y, 4), (w_z, 3), (w_a, 1), (w_y, 5), (w_z, 4), (w_a, 2), (w_b, 0), (w_z, 5),
             (w_a, 3), (w_b, 1), (w_a, 4), (w_b, 2), (w_a, 5), (w_b, 3), (w_b, 4), (w_b, 5)]
    for n, (f, p) in enumerate(order):
        f(p)
        if nb and n % 3 == 0 and n // 3 < nb:
            k = n // 3
            add_up(k, b_k)
            b_k = butterfly(k + 1) if k + 1 < nb else None
    store(r.sm.at[2 + nb], r.vectors)

    for c in sends:
        c.wait_send()
    sent_all(r.usend, us, 0)
    sent_all(r.usend, us, N - 1)
    sent_all(r.usend, us, 2 * (N - 1))
    for c in stores:
        c.wait()


def blend(old, new):
    return MOMENTUM * old + (1.0 - MOMENTUM) * new.astype(F32)


def local(mesh_shape, query_tokens, key_tokens, query_lengths, key_lengths, positives, key_queue, token_cotangent, heads_in,
          heads_bias, heads_out, expand_weight, expand_bias, shrink_weight, branch_bias, norm_gain, norm_shift,
          momentum_heads_in, momentum_heads_bias, momentum_heads_out, momentum_expand_weight, momentum_expand_bias,
          momentum_shrink_weight, momentum_branch_bias, momentum_norm_gain, momentum_norm_shift):
    DP = mesh_shape["dp"]
    L, D = query_tokens.shape
    HS, FS = heads_in.shape[2], expand_weight.shape[1]
    SH = D // DP
    N = DP * TENSOR
    PR = D // 2
    QN = key_queue.shape[0]
    gather = SH % 16 == 0 and (PR // DP) % 16 == 0
    RC = 128
    NCH = L // RC
    NZ = DP // 2
    t, dp = lax.axis_index("tensor"), lax.axis_index("dp")
    cfg = types.SimpleNamespace(D=D, HS=HS, FS=FS, L=L, DP=DP, SH=SH, RC=RC, gather=gather)

    vm = lambda shape, dtype: pltpu.VMEM(shape, dtype)
    any_, vmem, smem = (pl.BlockSpec(memory_space=m) for m in (pl.ANY, pltpu.VMEM, pltpu.SMEM))
    ins = [
        ("query_tokens", query_tokens, any_), ("key_tokens", key_tokens, any_),
        ("query_lengths", query_lengths, smem), ("key_lengths", key_lengths, smem), ("positives", positives, smem),
        ("key_queue", key_queue, any_), ("token_cotangent", token_cotangent, any_),
        ("heads_in", heads_in, any_), ("heads_bias", heads_bias, vmem), ("heads_out", heads_out, any_),
        ("expand_weight", expand_weight, any_), ("expand_bias", expand_bias.reshape(TENSOR, FS), vmem),
        ("shrink_weight", shrink_weight, any_), ("branch_bias", branch_bias, vmem), ("norm_gain", norm_gain, vmem),
        ("norm_shift", norm_shift, vmem), ("momentum_heads_bias", momentum_heads_bias, vmem),
        ("momentum_expand_bias", momentum_expand_bias.reshape(TENSOR, FS), vmem),
        ("momentum_branch_bias", momentum_branch_bias, vmem), ("momentum_norm_gain", momentum_norm_gain, vmem),
        ("momentum_norm_shift", momentum_norm_shift, vmem),
    ]
    outs = [
        ("query_output", (L, D), BF16), ("key_output", (L, D), BF16), ("input_gradient", (L, D), F32),
        ("grads", (PIECES, PR, D), BF16 if gather else F32), ("vectors", (16, D), F32),
    ]
    if gather:
        ins += [("momentum_heads_in", momentum_heads_in, any_), ("momentum_heads_out", momentum_heads_out, any_),
                ("momentum_expand_weight", momentum_expand_weight, any_),
                ("momentum_shrink_weight", momentum_shrink_weight, any_)]
        outs += [("o_heads_in", momentum_heads_in.shape, F32), ("o_heads_out", momentum_heads_out.shape, F32),
                 ("o_expand", momentum_expand_weight.shape, F32), ("o_shrink", momentum_shrink_weight.shape, F32)]
    else:
        updated = (
            blend(momentum_heads_in, lax.dynamic_slice_in_dim(heads_in, dp * SH, SH, 1)),
            blend(momentum_heads_out, lax.dynamic_slice_in_dim(heads_out, dp * SH, SH, 1)),
            blend(momentum_expand_weight, lax.dynamic_slice_in_dim(expand_weight, dp * SH, SH, 0)),
            blend(momentum_shrink_weight, lax.dynamic_slice_in_dim(shrink_weight, dp * SH, SH, 1)),
        )
        whole = lambda a, axis: lax.all_gather(a.astype(BF16), "dp", axis=axis, tiled=True)
        ins += [("key_heads", jnp.concatenate([whole(updated[0], 1), whole(updated[1].T, 0)[None]], axis=0), any_),
                ("key_ffn", jnp.stack([whole(updated[2], 0), whole(updated[3].T, 0)]), any_)]
    scratch = [
        ("X", vm((2, 2, L, D), BF16)), ("wqi", vm((2, 3, D, HS), BF16)), ("wo", vm((2, HS, D), BF16)),
        ("we", vm((2, D, FS), BF16)), ("ws", vm((2, FS, D), BF16)),
        ("wkh", vm((2, 4, D, HS), BF16)), ("wkf", vm((2, 2, D, FS), BF16)),
        ("queue", vm((QN, D), BF16)), ("cot", vm((L, D), BF16)),
        ("hb", vm((2, 4, HS), F32)), ("eb", vm((2, TENSOR, FS), F32)),
        ("qkv", vm((2, 3, 2, L, HS), BF16)), ("G", vm((2, 2, L, 128), F32)), ("C", vm((2, 2, L, HS), BF16)),
        ("U", vm((2, 2, L, D), BF16)), ("Uf", vm((2, L, D), F32)), ("H", vm((2, 2, L, FS), BF16)),
        ("slope", vm((2, 2, L, FS), BF16)), ("N1", vm((L, D), F32)), ("N2", vm((L, D), F32)),
        ("i1", vm((L, 128), F32)), ("i2", vm((L, 128), F32)), ("own", vm((2, L, D), F32)), ("part", vm((L, D), F32)),
        ("asend", vm((2, L, D), BF16)), ("arecv", vm((2, L, D), BF16)), ("fsend", vm((2, L, D), BF16)),
        ("frecv", vm((2, L, D), BF16)), ("oq", vm((L, D), BF16)), ("ok", vm((L, D), BF16)),
        ("usend", vm((2, 8, 128), F32)), ("units", vm((2, N, 8, 128), F32)), ("nsend", vm((N, 8, 128), F32)),
        ("nrecv", vm((N, 8, 128), F32)), ("d2", vm((L, D), F32)), ("dF", vm((2, L, D), BF16)),
        ("dZ", vm((2, 2, L, FS), BF16)), ("dusend", vm((L, D), BF16)), ("durecv", vm((L, D), BF16)),
        ("dA", vm((2, L, D), BF16)), ("dqkv", vm((2, 3, 2, L, HS), BF16)),
        ("dxsend", vm((L, D), BF16)), ("dxrecv", vm((L, D), BF16)),
        ("wsend", vm((PIECES, PR, D), BF16)), ("wrecv", vm((PIECES, PR, D), BF16)),
        ("sm", vm((3 + DP.bit_length(), 16, D), F32)), ("smx", vm((16, D), F32)),
        ("smr", vm((2 + DP.bit_length(), 16, D), F32)),
    ]
    if gather:
        scratch += [
            ("mhi", vm(momentum_heads_in.shape, F32)), ("mho", vm(momentum_heads_out.shape, F32)),
            ("mex", vm(momentum_expand_weight.shape, F32)), ("msh", vm(momentum_shrink_weight.shape, F32)),
            ("wacc", vm((PIECES, PR, D), BF16)), ("wyr", vm((PIECES, PR // 2, D), BF16)),
            ("wys", vm((PIECES, PR // 2, D), BF16)), ("wzr", vm((PIECES, NZ - 1, PR // DP, D), BF16)),
            ("wout", vm((PIECES, PR, D), BF16)),
        ]
    else:
        scratch += [("wacc32", vm((PIECES, PR, D), F32))]
    dma = pltpu.SemaphoreType.DMA
    nx = 2 + 6 * NCH + 4 * NCH
    ng = 2 * (NZ - 1) + 2 * NZ + 2
    nw = PIECES * (2 + 2 * (NZ - 1) + NZ)
    nv = 3 * (N - 1)
    for pair, count in ((("xs", "xr"), nx), (("cs", "cr"), 5), (("gs", "gr"), ng), (("us", "ur"), nv),
                        (("ws_s", "ws_r"), nw), (("bs", "br"), 2 + DP.bit_length())):
        for name in pair:
            scratch.append((name, dma((count,))))
    scratch += [("lsem", dma((16,))), ("ssem", dma((16,)))]
    cfg.names = [n for n, *_ in ins] + [n for n, *_ in outs] + [n for n, _ in scratch]

    def body(*refs):
        kernel(cfg, *refs)

    res = pl.pallas_call(
        body,
        out_shape=[jax.ShapeDtypeStruct(s, d) for _, s, d in outs],
        in_specs=[s for _, _, s in ins],
        out_specs=[any_] * len(outs),
        scratch_shapes=[s for _, s in scratch],
        compiler_params=pltpu.CompilerParams(collective_id=0, has_side_effects=True, vmem_limit_bytes=cfg_limit()),
        name="step",
    )(*[a for _, a, _ in ins])
    query_out, key_out, d_tokens, grads, vectors = res[:5]
    if gather:
        up_in, up_out, up_expand, up_shrink = res[5:]
    else:
        up_in, up_out, up_expand, up_shrink = updated
        grads, vectors = lax.psum((grads, jnp.concatenate([vectors])), "dp")
    g_shrink = grads[0:2].reshape(FS, D).astype(F32)
    g_expand = grads[2:4].reshape(D, FS).astype(F32)
    heads = grads[4:6].reshape(D, D)
    g_in = jnp.swapaxes(heads[: 3 * HS].reshape(3, HS, D), 1, 2).astype(F32)
    g_out = heads[3 * HS :].astype(F32)
    up_eb = blend(momentum_expand_bias, expand_bias)
    return (
        query_out, key_out, vectors[6, 0], d_tokens, g_in, vectors[9:11, :HS], g_out, g_expand, vectors[8, :FS], g_shrink,
        vectors[0:2], vectors[2:4], vectors[4:6], up_in, blend(momentum_heads_bias, heads_bias), up_out, up_expand,
        lax.dynamic_slice_in_dim(up_eb, t * FS, FS, 0), up_shrink, blend(momentum_branch_bias, branch_bias),
        blend(momentum_norm_gain, norm_gain), blend(momentum_norm_shift, norm_shift),
    )


def cfg_limit():
    return 64 * 1024 * 1024 - 4096


def solution(mesh):
    both = ("dp", "tensor")
    in_specs = (
        P(both, None), P(both, None), P("dp"), P("dp"), P(), P(both, None), P(both, None), P(None, None, "tensor"),
        P(None, "tensor"), P("tensor", None), P(None, "tensor"), P(), P("tensor", None), P(), P(), P(),
        P(None, "dp", "tensor"), P(None, "tensor"), P("tensor", "dp"), P("dp", "tensor"), P(), P("tensor", "dp"), P(), P(), P(),
    )
    out_specs = (
        P(both, None), P(both, None), P(), P(both, None), P(None, None, "tensor"), P(None, "tensor"), P("tensor", None),
        P(None, "tensor"), P("tensor"), P("tensor", None), P(), P(), P(), P(None, "dp", "tensor"), P(None, "tensor"),
        P("tensor", "dp"), P("dp", "tensor"), P("tensor"), P("tensor", "dp"), P(), P(), P(),
    )
    shape = dict(mesh.shape)
    return jax.shard_map(lambda *a: local(shape, *a), mesh=mesh, in_specs=in_specs, out_specs=out_specs, check_vma=False)
```

time: 996 us -> 248 us (0.25); the launches traced: 985 us -> 247 us
  waiting for transfers between devices: 501 us -> 0 us
  blocking collectives: 258 us -> 0 us
  Pallas kernels: 0 us -> 222 us
  other arithmetic: 84.6 us -> 8.92 us
  matrix products: 70.2 us -> 0 us
  local copies, waits for them, and re-layouts: 49.2 us -> 16 us
  between operations: 21.3 us -> 0.79 us
    pallas_call x0 -> x1, Pallas kernels: none -> 222 us  [local(): pl.pallas_call(body, out_shape=[jax.ShapeDtypeStruct(s, d) for _, s, d in...]
    psum x1 -> x0, waiting for transfers between devices: 164 us -> none  [backward(): lax.psum((grad_heads_in, grad_heads_bias, grad_heads_out, grad_expand, gr...]
    all_gather x4 -> x0, blocking collectives: 153 us -> none  [the longest x1 40.8 us: local(): lax.all_gather(query_unit.astype(jnp.bfloat16), ('dp', 'tensor'), axis=0,...]
    unnamed x17 -> x0, waiting for transfers between devices: 115 us -> none
    all_gather x8 -> x0, waiting for transfers between devices: 112 us -> none  [the longest x2 40.1 us: gather_grads(): return lax.all_gather(inputs, 'tensor', axis=0, tiled=True)]
    reduce_scatter x6 -> x0, waiting for transfers between devices: 109 us -> none  [the longest x4 80.8 us: sum_rows(): lax.psum_scatter(inputs.astype(jnp.bfloat16), 'tensor', scatter_dimension...]
    dot_general x25 -> x0, matrix products: 70.2 us -> none  [the longest x2 8.53 us: forward(): jnp.dot(hidden_low, shrink_weight, preferred_element_type=jnp.float32)]
    psum x2 -> x0, blocking collectives: 68.3 us -> none  [the longest x1 44.6 us: backward(): lax.psum((bias_pair, jnp.stack([gain_one, gain_two]), jnp.stack([shift_on...]
  transfers between devices with their start and end apart: 16 -> 0, of which waited for: 12 -> 0; matrix products, arithmetic and copies ran while one was open for 8% -> 0% of each run, Pallas kernels for 0% -> 0%
where the time goes in v1:
time: 248 us; the launch traced here: 247 us
  Pallas kernels  222 us (90%)
  local copies, waits for them, and re-layouts  16 us (6%)
  other arithmetic  8.92 us (4%)
    pallas_call x1, Pallas kernels, local(): pl.pallas_call(body, out_shape=[jax.ShapeDtypeStruct(s, d) for _, s, d in...  222 us
    unnamed x45, local copies, waits for them, and re-layouts  8.68 us

profile of v1, /device:TPU:0, one launch (start us, length us, event | category | flops | bytes accessed | tf_op | source)
XLA Modules:
  0.0 247.4 jit_solution(14519083531736518942)
XLA Ops:
  0.7 0.0 copy-start.6
  0.7 0.0 copy-start.11
  0.7 0.0 copy-start.15
  0.7 2.4 copy.47.refs_7_
  3.1 0.0 copy-done.6
  3.1 0.9 copy.48.refs_24_
  4.0 0.0 copy-done.11
  4.0 0.6 reshape.63.refs_17_
  4.6 0.0 copy-done.15
  4.6 0.6 reshape.62.refs_11_
  5.2 221.7 %step.1 = (bf16[256,768]{1,0:T(8,128)(2,1)}, bf16[256,768]{1,0:T(8,128)(2,1)}, f32[256,768]{1,0:T(8,128)}, bf16[6,384,768]{2,1,0:T(8,128)(2,1)}, f32[16,768]{1,0...) custom-call(bf16[256,768]{1,0:T(8,128)(2,1)} %refs_0_.1, ...), custom_call_target="tpu_custom_call" | custom-call | tf_op jit(solution)/shard_map/step/pallas_call | solution.py:836
  226.9 2.2 fusion.1
  229.1 0.0 copy-start.8
  229.1 0.0 copy-start.12
  229.1 2.7 %bitcast_convert_fusion = (f32[768,768]{1,0:T(8,128)}, f32[768,768]{1,0:T(8,128)}) fusion(bf16[2,384,768]{2,1,0:T(8,128)(2,1)S(1)} %get-tuple-element.62, bf16[2,384,768]{2,1,0:T(8,128)(2,1)S(1)} %get-tuple-element.63), kind=kLoop, calls=%fused_computation.1 | loop fusion | flops 1179648 | bytes 7077888 | tf_op jit(solution)/shard_map/convert_element_type | solution.py:851
  231.8 0.0 copy-done.8
  231.8 0.0 copy-done.12
  231.8 1.5 fusion.2
  233.3 0.1 slice.44
  233.4 0.0 copy-start.3
  233.4 1.4 convert_bitcast_fusion
  234.7 0.0 copy-start.9
  234.7 0.0 copy-start.10
  234.7 0.0 copy-start.13
  234.7 0.0 copy-start.14
  234.7 0.0 copy-start.16
  234.7 0.0 copy-start.17
  234.8 0.0 copy-start.2
  234.8 0.0 copy-start.1
  234.8 0.9 slice_convert_fusion
  235.6 0.0 copy-start
  235.6 1.4 slice_reduce_fusion
  237.0 1.3 slice.36
  238.3 1.2 slice.33
  239.5 0.0 copy-done.3
  239.5 0.9 copy.49
  240.4 1.4 fusion
  241.8 0.0 copy-done.9
  241.8 0.0 copy-done.10
  241.8 0.0 copy-done.13
  241.8 0.0 copy-done.14
  241.8 0.6 add_multiply_fusion
  242.4 0.0 copy-done.16
  242.4 0.0 copy-done.17
  242.4 0.6 add_multiply_fusion.3
  243.0 0.0 copy-done.2
  243.0 0.7 copy.56
  243.7 0.0 copy-done.1
  243.7 0.0 copy-start.5
  243.7 0.7 copy.57
  244.5 0.0 copy-done
  244.5 0.0 copy-start.7
  244.5 0.0 copy-start.4
  244.5 0.9 copy.58
  245.4 0.0 copy-done.5
  245.4 0.7 copy.59
  246.1 0.0 copy-done.7
  246.1 0.6 copy.60
  246.7 0.0 copy-done.4
  246.7 0.7 copy.61
Async XLA Ops:
  0.7 2.4 copy-start.6
  0.7 3.3 %copy-start.11 = (f32[3072]{0:T(1024)S(1)}, f32[3072]{0:T(1024)}, u32[]{:S(2)}) copy-start(f32[3072]{0:T(1024)} %param.45) | copy-start | bytes 36868
  0.7 3.9 %copy-start.15 = (bf16[3072]{0:T(1024)(128)(2,1)S(1)}, bf16[3072]{0:T(1024)(128)(2,1)}, u32[]{:S(2)}) copy-start(bf16[3072]{0:T(1024)(128)(2,1)} %param.36) | copy-start | bytes 18436
  229.1 2.7 %copy-start.8 = (f32[2,768]{1,0:T(2,128)S(1)}, f32[2,768]{1,0:T(2,128)}, u32[]{:S(2)}) copy-start(f32[2,768]{1,0:T(2,128)} %refs_18_.1) | copy-start | bytes 18436
  229.1 2.7 %copy-start.12 = (bf16[2,768]{1,0:T(2,128)(2,1)S(1)}, bf16[2,768]{1,0:T(2,128)(2,1)}, u32[]{:S(2)}) copy-start(bf16[2,768]{1,0:T(2,128)(2,1)} %refs_13_.1) | copy-start | bytes 9220
  233.4 6.2 %copy-start.3 = (f32[768,96]{1,0:T(8,128)S(1)}, f32[768,96]{1,0:T(8,128)}, u32[]{:S(2)}) copy-start(f32[768,96]{1,0:T(8,128)} %get-tuple-element.58) | copy-start | bytes 884740
  234.7 7.0 %copy-start.9 = (f32[2,768]{1,0:T(2,128)S(1)}, f32[2,768]{1,0:T(2,128)}, u32[]{:S(2)}) copy-start(f32[2,768]{1,0:T(2,128)} %refs_19_.1) | copy-start | bytes 18436
  234.7 7.0 %copy-start.10 = (f32[2,768]{1,0:T(2,128)S(1)}, f32[2,768]{1,0:T(2,128)}, u32[]{:S(2)}) copy-start(f32[2,768]{1,0:T(2,128)} %refs_20_.1) | copy-start | bytes 18436
  234.7 7.0 %copy-start.13 = (bf16[2,768]{1,0:T(2,128)(2,1)S(1)}, bf16[2,768]{1,0:T(2,128)(2,1)}, u32[]{:S(2)}) copy-start(bf16[2,768]{1,0:T(2,128)(2,1)} %refs_14_.1) | copy-start | bytes 9220
  234.7 7.1 %copy-start.14 = (bf16[2,768]{1,0:T(2,128)(2,1)S(1)}, bf16[2,768]{1,0:T(2,128)(2,1)}, u32[]{:S(2)}) copy-start(bf16[2,768]{1,0:T(2,128)(2,1)} %refs_15_.1) | copy-start | bytes 9220
  234.7 7.7 %copy-start.16 = (f32[2,192]{1,0:T(2,128)S(1)}, f32[2,192]{1,0:T(2,128)}, u32[]{:S(2)}) copy-start(f32[2,192]{1,0:T(2,128)} %refs_16_.1) | copy-start | bytes 4612
  234.7 7.7 %copy-start.17 = (bf16[2,192]{1,0:T(2,128)(2,1)S(1)}, bf16[2,192]{1,0:T(2,128)(2,1)}, u32[]{:S(2)}) copy-start(bf16[2,192]{1,0:T(2,128)(2,1)} %refs_8_.1) | copy-start | bytes 2308
  234.8 8.2 %copy-start.2 = (bf16[256,768]{1,0:T(8,128)(2,1)S(1)}, bf16[256,768]{1,0:T(8,128)(2,1)}, u32[]{:S(2)}) copy-start(bf16[256,768]{1,0:T(8,128)(2,1)} %get-tuple-element.95) | copy-start | bytes 1179652
  234.8 9.0 %copy-start.1 = (bf16[256,768]{1,0:T(8,128)(2,1)S(1)}, bf16[256,768]{1,0:T(8,128)(2,1)}, u32[]{:S(2)}) copy-start(bf16[256,768]{1,0:T(8,128)(2,1)} %get-tuple-element.96) | copy-start | bytes 1179652
  235.6 8.9 %copy-start = (f32[256,768]{1,0:T(8,128)S(1)}, f32[256,768]{1,0:T(8,128)}, u32[]{:S(2)}) copy-start(f32[256,768]{1,0:T(8,128)} %get-tuple-element.98) | copy-start | bytes 2359300
  243.7 1.6 copy-start.5
  244.5 1.6 copy-start.7
  244.5 2.2 copy-start.4
